TPU v7x, 32 devices: a whole 2x2x4 slice. The times are simulated.
32 devices in a mesh: grp: 2 (over y), row: 8 (over z, core), chan: 2 (over x).
Axes of the slice: x: 2, y: 2, z: 4, core: 2. Of those that a mesh axis runs over, the one named last changes fastest.
Arguments:
- pair: bfloat16 [1024, 512, 128], P(('grp', 'row'), 'chan'), parts along dimension 0, may hold values from -6 to 6
- pair_mask: int32 [1024, 512], P(('grp', 'row'), 'chan'), parts along dimension 0, may hold values 0 or 1
- chain_ids: int32 [1024], P('grp'), parts along dimension 0, may hold values from 0 to 5, never falling along the last dimension, each value on 1 to 128 neighbouring positions
- chain_embed: float32 [2, 128], replicated, may hold values from -4 to 4
- proj_weights: bfloat16 [2, 128, 512], replicated, may hold values from -0.5 to 0.5
- gate_weights: bfloat16 [2, 128, 128], replicated, may hold values from -0.5 to 0.5
- out_weights: bfloat16 [2, 128, 128], replicated, may hold values from -0.5 to 0.5
Outputs:
- updated: bfloat16 [1024, 512, 128], P(('grp', 'row'), 'chan'), parts along dimension 0
There are 2 independent parts, one for each index of `grp`. A program takes and returns all parts, laid end to end along the dimension named above; an argument that names none is the same for every part. Nothing has to cross between parts.
All inputs are finite; a program needn't handle non-finite values. No bound on the sum of `pair_mask` on one device may be relied on, other than what follows from the above.
Results may differ from a plain program's by a relative error of at most 0.0039.
Values may be sent and summed in bfloat16 or wider, within the bound.
No kernel may reach another device: no remote copies, remote signals or barrier semaphores. Data moves between devices by JAX's collectives and lax.ppermute only.
A program may use at most 128 MiB of HBM per device.

v0:
```python
import jax
import jax.numpy as jnp
from jax import lax
from jax.sharding import PartitionSpec as P


def layer_norm(values, axis):
    mean = jnp.mean(values, axis=axis, keepdims=True)
    centred = values - mean
    variance = jnp.mean(centred * centred, axis=axis, keepdims=True)
    return centred * lax.rsqrt(variance + 1e-05)


def to_channels(left, right):
    return (
        lax.all_to_all(
            lax.all_to_all(left, "chan", split_axis=0, concat_axis=2, tiled=True),
            "row",
            split_axis=0,
            concat_axis=1,
            tiled=True,
        ),
        lax.all_to_all(
            lax.all_to_all(right, "chan", split_axis=0, concat_axis=2, tiled=True),
            "row",
            split_axis=0,
            concat_axis=1,
            tiled=True,
        ),
    )


def to_pairs(mixed):
    return lax.all_to_all(
        lax.all_to_all(mixed, "row", split_axis=1, concat_axis=0, tiled=True),
        "chan",
        split_axis=2,
        concat_axis=0,
        tiled=True,
    )


def output_gate(normed, weight):
    return jax.nn.sigmoid(
        jnp.einsum("ijc,cd->ijd", normed, weight, preferred_element_type=jnp.float32)
    )


def local(pair, pair_mask, chain_ids, chain_embed, proj_weights, gate_weights, out_weights):
    tile_rows, tile_cols, feature_width = pair.shape
    hidden = proj_weights.shape[2] // 4
    row_start = lax.axis_index("row") * tile_rows
    col_start = lax.axis_index("chan") * tile_cols
    row_chain = lax.dynamic_slice_in_dim(chain_ids, row_start, tile_rows)
    col_chain = lax.dynamic_slice_in_dim(chain_ids, col_start, tile_cols)
    same_chain = row_chain[:, None] == col_chain[None, :]
    state = pair.astype(jnp.float32) + jnp.where(
        same_chain[..., None], chain_embed[1], chain_embed[0]
    )
    mask_values = pair_mask.astype(jnp.float32)[None, :, :]
    for update in range(2):
        normed = layer_norm(state, -1).astype(jnp.bfloat16)
        proj = jnp.einsum(
            "ijc,cd->dij", normed, proj_weights[update], preferred_element_type=jnp.float32
        )
        left = (jax.nn.sigmoid(proj[:hidden]) * proj[hidden : 2 * hidden] * mask_values).astype(
            jnp.bfloat16
        )
        right = (
            jax.nn.sigmoid(proj[2 * hidden : 3 * hidden]) * proj[3 * hidden :] * mask_values
        ).astype(jnp.bfloat16)
        left_full, right_full = to_channels(left, right)
        if update == 0:
            mixed = jnp.einsum(
                "cik,cjk->cij", left_full, right_full, preferred_element_type=jnp.float32
            )
        else:
            mixed = jnp.einsum(
                "cki,ckj->cij", left_full, right_full, preferred_element_type=jnp.float32
            )
        returned = to_pairs(mixed.astype(jnp.bfloat16))
        gate = output_gate(normed, gate_weights[update])
        mixnorm = layer_norm(returned.astype(jnp.float32), 0).astype(jnp.bfloat16)
        change = jnp.einsum(
            "dij,dc->ijc", mixnorm, out_weights[update], preferred_element_type=jnp.float32
        )
        state = state + gate * change
    return state.astype(jnp.bfloat16)


def solution(mesh):
    placed = (
        P(("grp", "row"), "chan", None),
        P(("grp", "row"), "chan"),
        P("grp"),
        P(),
        P(),
        P(),
        P(),
    )
    return jax.shard_map(
        local,
        mesh=mesh,
        in_specs=placed,
        out_specs=P(("grp", "row"), "chan", None),
        check_vma=False,
    )
```

profile of v0, /device:TPU:9, one launch (start us, length us, event | category | flops | bytes accessed | tf_op | source)
XLA Modules:
  0.0 1208.6 jit_solution(12476587920318128844)
XLA Ops:
  18.4 13.3 %convolution_bitcast_fusion.1 = f32[512,64,256]{0,2,1:T(8,128)} fusion(bf16[2,128,512]{2,1,0:T(8,128)(2,1)S(1)} %copy-done.5, bf16[64,256,128]{1,2,0:T(8,128)(2,1)S(1)} %copy-done, f32[64,256]{1,0:T(8,128)S(1)} %add_rsqrt_fusion.3, f32[64,256]{1,0:T(8,128)S(1)} %broadcast_multiply_fusion.3, f32[128]{0:T(128)S(1)} %get-tuple-element.10, ...), kind=kOutput, calls=%fused_computation.1 | convolution fusion | flops 2160066560 | bytes 38028288 | tf_op jit(solution)/shard_map/ijc,cd->dij/dot_general | solution.py:63
  31.7 15.4 %fusion.11 = (bf16[128,64,256]{0,2,1:T(8,128)(2,1)}, bf16[128,64,256]{0,2,1:T(8,128)(2,1)}) fusion(f32[512,64,256]{0,2,1:T(8,128)} %convolution_bitcast_fusion.1, f32[64,256]{1,0:T(8,128)S(1)} %convert_element_type.71), kind=kLoop, calls=%fused_computation.18 | loop fusion | flops 25165824 | bytes 42008576 | tf_op jit(solution)/shard_map/convert_element_type | solution.py:71
  66.3 40.0 %all-to-all-done = bf16[128,64,256]{2,1,0:T(8,128)(2,1)} async-done(((bf16[128,64,256]{2,1,0:T(8,128)(2,1)}), bf16[128,64,256]{2,1,0:T(8,128)(2,1)}, u32[]{:S(2)}, u32[]{:S(2)}) %all-to-all-start) | async-done | bytes 4194336 | tf_op jit(solution)/shard_map/all_to_all | solution.py:17
  116.5 41.3 %all-to-all-done.2 = bf16[128,64,256]{2,1,0:T(8,128)(2,1)} async-done(((bf16[128,64,256]{2,1,0:T(8,128)(2,1)}), bf16[128,64,256]{2,1,0:T(8,128)(2,1)}, u32[]{:S(2)}, u32[]{:S(2)}) %all-to-all-start.2) | async-done | bytes 4194336 | tf_op jit(solution)/shard_map/all_to_all | solution.py:24
  169.7 85.9 %all-to-all-done.1 = bf16[64,64,512]{2,1,0:T(8,128)(2,1)} async-done(((bf16[64,64,512]{2,1,0:T(8,128)(2,1)}), bf16[64,64,512]{2,1,0:T(8,128)(2,1)}, u32[]{:S(2)}, u32[]{:S(2)}) %all-to-all-start.1) | async-done | bytes 4194336 | tf_op jit(solution)/shard_map/all_to_all | solution.py:16
  255.7 8.4 all-to-all-start.3
  268.7 85.7 %all-to-all-done.3 = bf16[64,64,512]{2,1,0:T(8,128)(2,1)} async-done(((bf16[64,64,512]{2,1,0:T(8,128)(2,1)}), bf16[64,64,512]{2,1,0:T(8,128)(2,1)}, u32[]{:S(2)}, u32[]{:S(2)}) %all-to-all-start.3) | async-done | bytes 4194336 | tf_op jit(solution)/shard_map/all_to_all | solution.py:23
  362.7 97.1 %all_to_all.198 = bf16[8,512,512]{2,0,1:T(8,128)(2,1)S(1)} all-to-all(bf16[8,512,512]{2,0,1:T(8,128)(2,1)S(1)} %copy.154), channel_id=1, replica_groups=mesh['grp'=2,'row'=8,'chan'=2] {'row'}, dimensions={1} | all-to-all | bytes 8388608 | tf_op jit(solution)/shard_map/all_to_all | solution.py:35
  463.3 13.0 %copy.157 = bf16[64,64,512]{1,0,2:T(8,128)(2,1)} copy(bf16[64,64,512]{2,1,0:T(8,128)(2,1)} %bitcast.112) | data formatting | bytes 8388608 | tf_op jit(solution)/shard_map/all_to_all | solution.py:35
  476.3 10.1 reshape.90
  499.5 38.8 %all-to-all-done.5 = bf16[2,2,524288]{2,1,0:T(2,128)(2,1)} async-done(((bf16[2,2,524288]{2,1,0:T(2,128)(2,1)}), bf16[2,2,524288]{2,1,0:T(2,128)(2,1)}, u32[]{:S(2)}, u32[]{:S(2)}) %all-to-all-start.5) | async-done | bytes 4194336 | tf_op jit(solution)/shard_map/all_to_all | solution.py:34
  538.3 9.7 reshape.91
  548.0 9.7 copy.158
  557.7 18.1 %reshape.82 = f32[64,64,2,256]{3,2,1,0:T(2,128)} reshape(bf16[64,64,512]{2,1,0:T(8,128)(2,1)} %copy.158) | data formatting | bytes 12582912 | tf_op jit(solution)/shard_map/convert_element_type | solution.py:83
  588.7 10.1 multiply_convert_fusion.2
  613.9 13.2 %convolution_bitcast_fusion = f32[512,64,256]{0,2,1:T(8,128)} fusion(f32[64,256,128]{1,2,0:T(8,128)S(1)} %get-tuple-element.12, f32[64,256]{1,0:T(8,128)S(1)} %add_rsqrt_fusion.1, f32[64,256]{1,0:T(8,128)S(1)} %broadcast_multiply_fusion.1, bf16[2,128,512]{2,1,0:T(8,128)(2,1)S(1)} %copy-done.5), kind=kOutput, calls=%fused_computation | convolution fusion | flops 2153775104 | bytes 42205184 | tf_op jit(solution)/shard_map/ijc,cd->dij/dot_general | solution.py:63
  627.1 15.4 %fusion.1 = (bf16[128,64,256]{0,2,1:T(8,128)(2,1)}, bf16[128,64,256]{0,2,1:T(8,128)(2,1)}) fusion(f32[512,64,256]{0,2,1:T(8,128)} %convolution_bitcast_fusion, f32[64,256]{1,0:T(8,128)S(1)} %convert_element_type.71), kind=kLoop, calls=%fused_computation.4 | loop fusion | flops 25165824 | bytes 42008576 | tf_op jit(solution)/shard_map/convert_element_type | solution.py:71
  661.7 38.5 %all-to-all-done.6 = bf16[128,64,256]{2,1,0:T(8,128)(2,1)} async-done(((bf16[128,64,256]{2,1,0:T(8,128)(2,1)}), bf16[128,64,256]{2,1,0:T(8,128)(2,1)}, u32[]{:S(2)}, u32[]{:S(2)}) %all-to-all-start.6) | async-done | bytes 4194336 | tf_op jit(solution)/shard_map/all_to_all | solution.py:17
  710.4 39.9 %all-to-all-done.8 = bf16[128,64,256]{2,1,0:T(8,128)(2,1)} async-done(((bf16[128,64,256]{2,1,0:T(8,128)(2,1)}), bf16[128,64,256]{2,1,0:T(8,128)(2,1)}, u32[]{:S(2)}, u32[]{:S(2)}) %all-to-all-start.8) | async-done | bytes 4194336 | tf_op jit(solution)/shard_map/all_to_all | solution.py:24
  750.3 10.5 all-to-all-start.7
  765.4 85.9 %all-to-all-done.7 = bf16[64,64,512]{2,1,0:T(8,128)(2,1)} async-done(((bf16[64,64,512]{2,1,0:T(8,128)(2,1)}), bf16[64,64,512]{2,1,0:T(8,128)(2,1)}, u32[]{:S(2)}, u32[]{:S(2)}) %all-to-all-start.7) | async-done | bytes 4194336 | tf_op jit(solution)/shard_map/all_to_all | solution.py:16
  851.3 8.3 all-to-all-start.9
  864.3 85.7 %all-to-all-done.9 = bf16[64,64,512]{2,1,0:T(8,128)(2,1)} async-done(((bf16[64,64,512]{2,1,0:T(8,128)(2,1)}), bf16[64,64,512]{2,1,0:T(8,128)(2,1)}, u32[]{:S(2)}, u32[]{:S(2)}) %all-to-all-start.9) | async-done | bytes 4194336 | tf_op jit(solution)/shard_map/all_to_all | solution.py:23
  958.2 97.1 %all_to_all.199 = bf16[8,512,512]{2,0,1:T(8,128)(2,1)S(1)} all-to-all(bf16[8,512,512]{2,0,1:T(8,128)(2,1)S(1)} %copy.172), channel_id=1, replica_groups=mesh['grp'=2,'row'=8,'chan'=2] {'row'}, dimensions={1} | all-to-all | bytes 8388608 | tf_op jit(solution)/shard_map/all_to_all | solution.py:35
  1058.9 13.0 %copy.175 = bf16[64,64,512]{1,0,2:T(8,128)(2,1)} copy(bf16[64,64,512]{2,1,0:T(8,128)(2,1)} %bitcast.113) | data formatting | bytes 8388608 | tf_op jit(solution)/shard_map/all_to_all | solution.py:35
  1071.9 10.0 reshape.92
  1095.5 38.4 %all-to-all-done.11 = bf16[2,2,524288]{2,1,0:T(2,128)(2,1)} async-done(((bf16[2,2,524288]{2,1,0:T(2,128)(2,1)}), bf16[2,2,524288]{2,1,0:T(2,128)(2,1)}, u32[]{:S(2)}, u32[]{:S(2)}) %all-to-all-start.11) | async-done | bytes 4194336 | tf_op jit(solution)/shard_map/all_to_all | solution.py:34
  1133.8 9.7 reshape.93
  1143.6 9.7 copy.176
  1153.3 9.8 reshape.83
  1176.0 10.1 multiply_convert_fusion
  1193.0 8.8 add_convert_fusion
  (70 shorter events, 207.2 us)
Async XLA Ops:
  2.3 16.1 %copy-start.7 = (s32[64,256]{1,0:T(8,128)S(1)}, s32[64,256]{1,0:T(8,128)}, u32[]{:S(2)}) copy-start(s32[64,256]{1,0:T(8,128)} %param.8) | copy-start | bytes 196612
  2.3 16.1 %copy-start.5 = (bf16[2,128,512]{2,1,0:T(8,128)(2,1)S(1)}, bf16[2,128,512]{2,1,0:T(8,128)(2,1)}, u32[]{:S(2)}) copy-start(bf16[2,128,512]{2,1,0:T(8,128)(2,1)} %param.11) | copy-start | bytes 786436
  8.7 9.7 copy-start
  53.9 52.4 %all-to-all-start = ((bf16[128,64,256]{2,1,0:T(8,128)(2,1)}), bf16[128,64,256]{2,1,0:T(8,128)(2,1)}, u32[]{:S(2)}, u32[]{:S(2)}) async-start(bf16[128,64,256]{2,1,0:T(8,128)(2,1)} %copy.148), calls=%async_computation | async-start | bytes 8388608 | tf_op jit(solution)/shard_map/all_to_all | solution.py:17
  106.3 51.5 %all-to-all-start.2 = ((bf16[128,64,256]{2,1,0:T(8,128)(2,1)}), bf16[128,64,256]{2,1,0:T(8,128)(2,1)}, u32[]{:S(2)}, u32[]{:S(2)}) async-start(bf16[128,64,256]{2,1,0:T(8,128)(2,1)} %copy.151), calls=%async_computation.2 | async-start | bytes 8388608 | tf_op jit(solution)/shard_map/all_to_all | solution.py:24
  157.8 97.9 %all-to-all-start.1 = ((bf16[64,64,512]{2,1,0:T(8,128)(2,1)}), bf16[64,64,512]{2,1,0:T(8,128)(2,1)}, u32[]{:S(2)}, u32[]{:S(2)}) async-start(bf16[64,64,512]{2,1,0:T(8,128)(2,1)} %bitcast.114), calls=%async_computation.1 | async-start | bytes 8388608 | tf_op jit(solution)/shard_map/all_to_all | solution.py:16
  255.7 98.8 %all-to-all-start.3 = ((bf16[64,64,512]{2,1,0:T(8,128)(2,1)}), bf16[64,64,512]{2,1,0:T(8,128)(2,1)}, u32[]{:S(2)}, u32[]{:S(2)}) async-start(bf16[64,64,512]{2,1,0:T(8,128)(2,1)} %bitcast.115), calls=%async_computation.3 | async-start | bytes 8388608 | tf_op jit(solution)/shard_map/all_to_all | solution.py:23
  354.5 3.4 copy-start.3
  476.3 15.7 %copy-start.6 = (bf16[2,128,128]{2,1,0:T(8,128)(2,1)S(1)}, bf16[2,128,128]{2,1,0:T(8,128)(2,1)}, u32[]{:S(2)}) copy-start(bf16[2,128,128]{2,1,0:T(8,128)(2,1)} %param.12) | copy-start | bytes 196612
  486.4 51.9 %all-to-all-start.5 = ((bf16[2,2,524288]{2,1,0:T(2,128)(2,1)}), bf16[2,2,524288]{2,1,0:T(2,128)(2,1)}, u32[]{:S(2)}, u32[]{:S(2)}) async-start(bf16[2,2,524288]{2,1,0:T(2,128)(2,1)} %reshape.90), calls=%async_computation.5 | async-start | bytes 8388608 | tf_op jit(solution)/shard_map/all_to_all | solution.py:34
  588.7 17.4 %copy-start.8 = (bf16[2,128,128]{2,1,0:T(8,128)(2,1)S(1)}, bf16[2,128,128]{2,1,0:T(8,128)(2,1)}, u32[]{:S(2)}) copy-start(bf16[2,128,128]{2,1,0:T(8,128)(2,1)} %param.13) | copy-start | bytes 196612
  598.8 7.3 copy-start.1
  612.1 15.0 %copy-start.2 = (f32[64,256,128]{1,2,0:T(8,128)}, f32[64,256,128]{1,2,0:T(8,128)S(1)}, u32[]{:S(2)}) copy-start(f32[64,256,128]{1,2,0:T(8,128)S(1)} %get-tuple-element.12) | copy-start | bytes 25165828
  649.2 51.0 %all-to-all-start.6 = ((bf16[128,64,256]{2,1,0:T(8,128)(2,1)}), bf16[128,64,256]{2,1,0:T(8,128)(2,1)}, u32[]{:S(2)}, u32[]{:S(2)}) async-start(bf16[128,64,256]{2,1,0:T(8,128)(2,1)} %copy.165), calls=%async_computation.6 | async-start | bytes 8388608 | tf_op jit(solution)/shard_map/all_to_all | solution.py:17
  700.2 50.1 %all-to-all-start.8 = ((bf16[128,64,256]{2,1,0:T(8,128)(2,1)}), bf16[128,64,256]{2,1,0:T(8,128)(2,1)}, u32[]{:S(2)}, u32[]{:S(2)}) async-start(bf16[128,64,256]{2,1,0:T(8,128)(2,1)} %copy.168), calls=%async_computation.8 | async-start | bytes 8388608 | tf_op jit(solution)/shard_map/all_to_all | solution.py:24
  750.3 101.0 %all-to-all-start.7 = ((bf16[64,64,512]{2,1,0:T(8,128)(2,1)}), bf16[64,64,512]{2,1,0:T(8,128)(2,1)}, u32[]{:S(2)}, u32[]{:S(2)}) async-start(bf16[64,64,512]{2,1,0:T(8,128)(2,1)} %bitcast.116), calls=%async_computation.7 | async-start | bytes 8388608 | tf_op jit(solution)/shard_map/all_to_all | solution.py:16
  851.3 98.7 %all-to-all-start.9 = ((bf16[64,64,512]{2,1,0:T(8,128)(2,1)}), bf16[64,64,512]{2,1,0:T(8,128)(2,1)}, u32[]{:S(2)}, u32[]{:S(2)}) async-start(bf16[64,64,512]{2,1,0:T(8,128)(2,1)} %bitcast.117), calls=%async_computation.9 | async-start | bytes 8388608 | tf_op jit(solution)/shard_map/all_to_all | solution.py:23
  950.0 3.4 copy-start.4
  1081.9 51.9 %all-to-all-start.11 = ((bf16[2,2,524288]{2,1,0:T(2,128)(2,1)}), bf16[2,2,524288]{2,1,0:T(2,128)(2,1)}, u32[]{:S(2)}, u32[]{:S(2)}) async-start(bf16[2,2,524288]{2,1,0:T(2,128)(2,1)} %reshape.92), calls=%async_computation.11 | async-start | bytes 8388608 | tf_op jit(solution)/shard_map/all_to_all | solution.py:34
where the time goes:
time: 1230 us; the launch traced here: 1210 us
  waiting for transfers between devices  580 us (47%)
  local copies, waits for them, and re-layouts  216 us (18%)
  blocking collectives  194 us (16%)
  other arithmetic  87.9 us (7%)
  starting transfers between devices  68.2 us (6%)
  matrix products  61.5 us (5%)
    all_to_all x2, blocking collectives, to_pairs(): lax.all_to_all(mixed, 'row', split_axis=1, concat_axis=0, tiled=True)  194 us
    all_to_all x2, waiting for transfers between devices, to_channels(): lax.all_to_all(lax.all_to_all(left, 'chan', split_axis=0, concat_axis=2,...  172 us
    all_to_all x2, waiting for transfers between devices, to_channels(): lax.all_to_all(lax.all_to_all(right, 'chan', split_axis=0, concat_axis=2,...  171 us
    all_to_all x2, waiting for transfers between devices, to_channels(): lax.all_to_all(right, 'chan', split_axis=0, concat_axis=2, tiled=True)  81.2 us
    all_to_all x2, waiting for transfers between devices, to_channels(): lax.all_to_all(left, 'chan', split_axis=0, concat_axis=2, tiled=True)  78.5 us
    all_to_all x2, waiting for transfers between devices, to_pairs(): lax.all_to_all(lax.all_to_all(mixed, 'row', split_axis=1, concat_axis=0,...  77.2 us
    unnamed x23, local copies, waits for them, and re-layouts  47.7 us
    convert_element_type x4, local copies, waits for them, and re-layouts, local(): mixnorm = layer_norm(returned.astype(jnp.float32), 0).astype(jnp.bfloat16)  42.2 us
  transfers between devices with their start and end apart: 10, of which 10 were waited for; matrix products, arithmetic and copies ran while one was open for 5% of the time, Pallas kernels for 0%

commit v1 on v0

v1 whole, which is shorter than its diff:
```python
import functools

import jax
import jax.numpy as jnp
from jax import lax
from jax.experimental import pallas as pl
from jax.experimental.pallas import tpu as pltpu
from jax.sharding import PartitionSpec as P

EPS = 1e-05
LANES = 128
VMEM = 56 * 1024 * 1024


def sigmoid(x):
    return 0.5 * jnp.tanh(0.5 * x) + 0.5


def norm_channels(values):
    scale = 1.0 / values.shape[0]
    mean = jnp.sum(values, axis=0, keepdims=True) * scale
    centred = values - mean
    variance = jnp.sum(centred * centred, axis=0, keepdims=True) * scale
    return centred * lax.rsqrt(variance + EPS)


def dot(a, b):
    return jnp.dot(a, b, preferred_element_type=jnp.float32)


def first_state(pair_ref, same_row, embed_ref, eye_ref, i):
    turned = lax.dot_general(
        eye_ref[...], pair_ref[i], (((1,), (1,)), ((), ())), preferred_element_type=jnp.float32
    )
    return turned + jnp.where(same_row, embed_ref[:, 1:2], embed_ref[:, 0:1])


def put_row(scratch, i, rows, values):
    for part in range(values.shape[1] // LANES):
        scratch[part, pl.ds(i, values.shape[0], stride=rows), :] = values[
            :, part * LANES : (part + 1) * LANES
        ]


def get_row(scratch, i, rows, channels):
    return jnp.concatenate(
        [scratch[part, pl.ds(i, channels, stride=rows), :] for part in range(scratch.shape[0])],
        axis=1,
    )


def project_row(normed, mask_row, weight_ref, left_scr, right_scr, i, rows):
    hidden = weight_ref.shape[0] // 4
    proj = dot(weight_ref[...], normed)
    put_row(left_scr, i, rows, sigmoid(proj[:hidden]) * proj[hidden : 2 * hidden] * mask_row)
    put_row(
        right_scr, i, rows, sigmoid(proj[2 * hidden : 3 * hidden]) * proj[3 * hidden :] * mask_row
    )


def write_sides(left_scr, right_scr, out_ref):
    targets, _, share, rows, cols = out_ref.shape
    for side, scratch in enumerate((left_scr, right_scr)):
        for part in range(cols // LANES):
            out_ref[:, side, :, :, part * LANES : (part + 1) * LANES] = (
                scratch[part].astype(jnp.bfloat16).reshape(targets, share, rows, LANES)
            )


def read_mixed(mixed_ref, scratch):
    for part in range(scratch.shape[0]):
        scratch[part] = (
            mixed_ref[:, :, part * LANES : (part + 1) * LANES]
            .astype(jnp.float32)
            .reshape(scratch.shape[1:])
        )


def start_kernel(
    row_chain, pair_ref, mask_ref, col_chain, embed_ref, eye_ref, proj_ref, out_ref, left_scr, right_scr
):
    rows = pair_ref.shape[0]
    step = pl.program_id(0)

    @pl.loop(0, rows)
    def _(i):
        same = col_chain[...] == row_chain[step * rows + i]
        state = first_state(pair_ref, same, embed_ref, eye_ref, i)
        normed = norm_channels(state).astype(jnp.bfloat16)
        mask_row = mask_ref[pl.ds(i, 1), :].astype(jnp.float32)
        project_row(normed, mask_row, proj_ref, left_scr, right_scr, i, rows)

    write_sides(left_scr, right_scr, out_ref)


def middle_kernel(
    row_chain, mixed_ref, pair_ref, mask_ref, col_chain, embed_ref, eye_ref, gate_ref, back_ref, proj_ref,
    state_ref, out_ref, mixed_scr, left_scr, right_scr,
):
    rows = pair_ref.shape[0]
    channels = mixed_ref.shape[0]
    step = pl.program_id(0)
    read_mixed(mixed_ref, mixed_scr)

    @pl.loop(0, rows)
    def _(i):
        same = col_chain[...] == row_chain[step * rows + i]
        state = first_state(pair_ref, same, embed_ref, eye_ref, i)
        normed = norm_channels(state).astype(jnp.bfloat16)
        gate = sigmoid(dot(gate_ref[...], normed))
        mixnorm = norm_channels(get_row(mixed_scr, i, rows, channels)).astype(jnp.bfloat16)
        state = state + gate * dot(back_ref[...], mixnorm)
        state_ref[i] = state
        normed = norm_channels(state).astype(jnp.bfloat16)
        mask_row = mask_ref[pl.ds(i, 1), :].astype(jnp.float32)
        project_row(normed, mask_row, proj_ref, left_scr, right_scr, i, rows)

    write_sides(left_scr, right_scr, out_ref)


def end_kernel(mixed_ref, state_ref, gate_ref, back_ref, out_ref, mixed_scr):
    rows = state_ref.shape[0]
    channels = mixed_ref.shape[0]
    read_mixed(mixed_ref, mixed_scr)

    @pl.loop(0, rows)
    def _(i):
        state = state_ref[i]
        normed = norm_channels(state).astype(jnp.bfloat16)
        gate = sigmoid(dot(gate_ref[...], normed))
        mixnorm = norm_channels(get_row(mixed_scr, i, rows, channels)).astype(jnp.bfloat16)
        state = state + gate * dot(back_ref[...], mixnorm)
        out_ref[i] = state.T.astype(jnp.bfloat16)


def whole(array):
    return pl.BlockSpec(array.shape, lambda *_: (0,) * array.ndim)


def params():
    return pltpu.CompilerParams(vmem_limit_bytes=VMEM)


def scratches(count, channels, rows, cols):
    return [pltpu.VMEM((cols // LANES, channels * rows, LANES), jnp.float32)] * count


SMEM_SPEC = pl.BlockSpec(memory_space=pltpu.SMEM)


def start_call(row_chain, pair, mask, col_chain, embed, eye, proj, targets, block):
    rows, cols, width = pair.shape
    hidden = proj.shape[0] // 4
    share = hidden // targets
    return pl.pallas_call(
        start_kernel,
        grid=(rows // block,),
        in_specs=[
            SMEM_SPEC,
            pl.BlockSpec((block, cols, width), lambda s: (s, 0, 0)),
            pl.BlockSpec((block, cols), lambda s: (s, 0)),
            whole(col_chain),
            whole(embed),
            whole(eye),
            whole(proj),
        ],
        out_specs=pl.BlockSpec((targets, 2, share, block, cols), lambda s: (0, 0, 0, s, 0)),
        out_shape=jax.ShapeDtypeStruct((targets, 2, share, rows, cols), jnp.bfloat16),
        scratch_shapes=scratches(2, hidden, block, cols),
        compiler_params=params(),
    )(row_chain, pair, mask, col_chain, embed, eye, proj)


def middle_call(row_chain, mixed, pair, mask, col_chain, embed, eye, gate, back, proj, targets, block):
    rows, cols, width = pair.shape
    hidden = proj.shape[0] // 4
    share = hidden // targets
    return pl.pallas_call(
        middle_kernel,
        grid=(rows // block,),
        in_specs=[
            SMEM_SPEC,
            pl.BlockSpec((hidden, block, cols), lambda s: (0, s, 0)),
            pl.BlockSpec((block, cols, width), lambda s: (s, 0, 0)),
            pl.BlockSpec((block, cols), lambda s: (s, 0)),
            whole(col_chain),
            whole(embed),
            whole(eye),
            whole(gate),
            whole(back),
            whole(proj),
        ],
        out_specs=[
            pl.BlockSpec((block, width, cols), lambda s: (s, 0, 0)),
            pl.BlockSpec((targets, 2, share, block, cols), lambda s: (0, 0, 0, s, 0)),
        ],
        out_shape=[
            jax.ShapeDtypeStruct((rows, width, cols), jnp.float32),
            jax.ShapeDtypeStruct((targets, 2, share, rows, cols), jnp.bfloat16),
        ],
        scratch_shapes=scratches(3, hidden, block, cols),
        compiler_params=params(),
    )(row_chain, mixed, pair, mask, col_chain, embed, eye, gate, back, proj)


def end_call(mixed, state, gate, back, block):
    rows, width, cols = state.shape
    hidden = mixed.shape[0]
    return pl.pallas_call(
        end_kernel,
        grid=(rows // block,),
        in_specs=[
            pl.BlockSpec((hidden, block, cols), lambda s: (0, s, 0)),
            pl.BlockSpec((block, width, cols), lambda s: (s, 0, 0)),
            whole(gate),
            whole(back),
        ],
        out_specs=pl.BlockSpec((block, cols, width), lambda s: (s, 0, 0)),
        out_shape=jax.ShapeDtypeStruct((rows, cols, width), jnp.bfloat16),
        scratch_shapes=scratches(1, hidden, block, cols),
        compiler_params=params(),
    )(mixed, state, gate, back)


def product_kernel(update, sides_ref, out_ref):
    row_parts, col_parts, _, _, rows, cols = sides_ref.shape
    size = row_parts * rows

    def side(which, part):
        return sides_ref[:, part, which, 0].reshape(size, cols)

    if update == 0:
        total = None
        for part in range(col_parts):
            term = lax.dot_general(
                side(0, part), side(1, part), (((1,), (1,)), ((), ())),
                preferred_element_type=jnp.float32,
            )
            total = term if total is None else total + term
        mixed = total.astype(jnp.bfloat16)
        for part in range(col_parts):
            out_ref[:, part, 0] = mixed[:, part * cols : (part + 1) * cols].reshape(
                row_parts, rows, cols
            )
    else:
        left = jnp.concatenate([side(0, part) for part in range(col_parts)], axis=1)
        for part in range(col_parts):
            mixed = lax.dot_general(
                left, side(1, part), (((0,), (0,)), ((), ())), preferred_element_type=jnp.float32
            ).astype(jnp.bfloat16)
            out_ref[:, part, 0] = mixed.reshape(row_parts, rows, cols)


def product_call(sides, update, row_parts, col_parts):
    targets, _, share, rows, cols = sides.shape
    sides = sides.reshape(row_parts, col_parts, 2, share, rows, cols)
    out = pl.pallas_call(
        functools.partial(product_kernel, update),
        grid=(share,),
        in_specs=[
            pl.BlockSpec((row_parts, col_parts, 2, 1, rows, cols), lambda s: (0, 0, 0, s, 0, 0))
        ],
        out_specs=pl.BlockSpec((row_parts, col_parts, 1, rows, cols), lambda s: (0, 0, s, 0, 0)),
        out_shape=jax.ShapeDtypeStruct((row_parts, col_parts, share, rows, cols), jnp.bfloat16),
        compiler_params=params(),
    )(sides)
    return out.reshape(targets, share, rows, cols)


def exchange(array):
    return lax.all_to_all(array, ("row", "chan"), split_axis=0, concat_axis=0, tiled=True)


def local(mesh, pair, pair_mask, chain_ids, chain_embed, proj_weights, gate_weights, out_weights):
    rows, cols, width = pair.shape
    row_parts, col_parts = mesh.shape["row"], mesh.shape["chan"]
    targets = row_parts * col_parts
    hidden = out_weights.shape[1]
    block = 16
    row_chain = lax.dynamic_slice_in_dim(chain_ids, lax.axis_index("row") * rows, rows)
    col_chain = lax.dynamic_slice_in_dim(chain_ids, lax.axis_index("chan") * cols, cols)[None, :]
    embed = chain_embed.T
    eye = jnp.eye(width, dtype=jnp.bfloat16)
    proj, gate, back = (
        jnp.swapaxes(weight, 1, 2) for weight in (proj_weights, gate_weights, out_weights)
    )

    sides = start_call(row_chain, pair, pair_mask, col_chain, embed, eye, proj[0], targets, block)
    mixed = exchange(product_call(exchange(sides), 0, row_parts, col_parts))
    state, sides = middle_call(
        row_chain, mixed.reshape(hidden, rows, cols), pair, pair_mask, col_chain, embed, eye,
        gate[0], back[0], proj[1], targets, block,
    )
    mixed = exchange(product_call(exchange(sides), 1, row_parts, col_parts))
    return end_call(mixed.reshape(hidden, rows, cols), state, gate[1], back[1], block)


def solution(mesh):
    placed = (
        P(("grp", "row"), "chan", None),
        P(("grp", "row"), "chan"),
        P("grp"),
        P(),
        P(),
        P(),
        P(),
    )
    return jax.shard_map(
        functools.partial(local, mesh),
        mesh=mesh,
        in_specs=placed,
        out_specs=P(("grp", "row"), "chan", None),
        check_vma=False,
    )
```

time: 1230 us -> 721 us (0.59); the launches traced: 1210 us -> 720 us
  waiting for transfers between devices: 580 us -> 92.4 us
  blocking collectives: 194 us -> 475 us
  local copies, waits for them, and re-layouts: 216 us -> 6.79 us
  Pallas kernels: 0 us -> 140 us
  other arithmetic: 87.9 us -> 0.63 us
  starting transfers between devices: 68.2 us -> 4.59 us
  matrix products: 61.5 us -> 0 us
    all_to_all x10 -> x1, waiting for transfers between devices: 580 us -> 92.4 us  [exchange(): lax.all_to_all(array, ('row', 'chan'), split_axis=0, concat_axis=0, tiled...]
    all_to_all x2 -> x3, blocking collectives: 194 us -> 475 us  [exchange(): lax.all_to_all(array, ('row', 'chan'), split_axis=0, concat_axis=0, tiled...]
    pallas_call x0 -> x5, Pallas kernels: none -> 140 us  [the longest x1 56.9 us: middle_call(): pl.pallas_call(middle_kernel, grid=(rows // block,), in_specs=[SMEM_SPEC,...]
    all_to_all x14 -> x0, local copies, waits for them, and re-layouts: 85.4 us -> none  [the longest x4 33.1 us: to_pairs(): lax.all_to_all(mixed, 'row', split_axis=1, concat_axis=0, tiled=True)]
    convert_element_type x11 -> x0, local copies, waits for them, and re-layouts: 80.6 us -> none  [the longest x4 42.2 us: local(): mixnorm = layer_norm(returned.astype(jnp.float32), 0).astype(jnp.bfloat16)]
    all_to_all x10 -> x1, starting transfers between devices: 68.2 us -> 4.59 us  [exchange(): lax.all_to_all(array, ('row', 'chan'), split_axis=0, concat_axis=0, tiled...]
    dot_general x8 -> x0, matrix products: 61.5 us -> none  [the longest x2 26.5 us: local(): jnp.einsum('ijc,cd->dij', normed, proj_weights[update], preferred_element...]
    convert_element_type x5 -> x1, other arithmetic: 50.9 us -> 0.63 us  [local(): eye = jnp.eye(width, dtype=jnp.bfloat16)]
  transfers between devices with their start and end apart: 10 -> 1, of which waited for: 10 -> 1; matrix products, arithmetic and copies ran while one was open for 5% -> 0% of each run, Pallas kernels for 0% -> 0%
where the time goes in v1:
time: 721 us; the launch traced here: 720 us
  blocking collectives  475 us (66%)
  Pallas kernels  140 us (19%)
  waiting for transfers between devices  92.4 us (13%)
    all_to_all x3, blocking collectives, exchange(): lax.all_to_all(array, ('row', 'chan'), split_axis=0, concat_axis=0, tiled...  475 us
    all_to_all x1, waiting for transfers between devices, exchange(): lax.all_to_all(array, ('row', 'chan'), split_axis=0, concat_axis=0, tiled...  92.4 us
    pallas_call x1, Pallas kernels, middle_call(): pl.pallas_call(middle_kernel, grid=(rows // block,), in_specs=[SMEM_SPEC,...  56.9 us
    pallas_call x1, Pallas kernels, start_call(): pl.pallas_call(start_kernel, grid=(rows // block,), in_specs=[SMEM_SPEC,...  38.7 us
    pallas_call x1, Pallas kernels, end_call(): pl.pallas_call(end_kernel, grid=(rows // block,), in_specs=[pl.BlockSpec(...  26.8 us
    pallas_call x2, Pallas kernels, product_call(): pl.pallas_call(functools.partial(product_kernel, update), grid=(share,),...  18 us
  transfers between devices with their start and end apart: 1, of which 1 were waited for; matrix products, arithmetic and copies ran while one was open for 0% of the time, Pallas kernels for 0%

profile of v1, /device:TPU:9, one launch (start us, length us, event | category | flops | bytes accessed | tf_op | source)
XLA Modules:
  0.0 719.7 jit_solution(16903913212080438394)
XLA Ops:
  0.0 0.6 fusion.eye_ref
  0.6 1.3 dynamic_slice.6.row_chain
  1.9 1.3 dynamic_slice.7
  3.3 1.4 copy.8
  4.7 1.1 copy.9
  5.8 0.7 slice_bitcast_fusion
  6.5 38.7 %shard_map.73 = bf16[16,2,8,64,256]{4,3,2,1,0:T(8,128)(2,1)} custom-call(s32[64]{0:T(128)} %dynamic_slice.6.row_chain, bf16[64,256,128]{2,1,0:T(8,128)(2,1)} %pair_ref.3, s32[64,256]{1,0:T(8,128)} %mask_ref.3, s32[1,256]{1,0:T(1,128)} %bitcast.33, f32[128,2]{1,0:T(8,128)} %bitcast.29, bf16[128,128]{1,0:T(8,128)(2,1)} %fusion.eye_ref, ...), custom_call_target="tpu_custom_call" | custom-call | tf_op jit(solution)/shard_map/pallas_call | solution.py:155
  45.2 189.7 %all_to_all.20 = bf16[16,2,8,64,256]{4,3,2,1,0:T(8,128)(2,1)} all-to-all(bf16[16,2,8,64,256]{4,3,2,1,0:T(8,128)(2,1)} %shard_map.73), channel_id=1, replica_groups=mesh['grp'=2,'row'=8,'chan'=2] {'row','chan'}, dimensions={0} | all-to-all | bytes 16777216 | tf_op jit(solution)/shard_map/all_to_all | solution.py:271
  234.9 9.0 %shard_map.74 = bf16[8,2,8,64,256]{4,3,2,1,0:T(8,128)(2,1)} custom-call(bf16[8,2,2,8,64,256]{5,4,3,2,1,0:T(8,128)(2,1)} %bitcast.23), custom_call_target="tpu_custom_call" | custom-call | tf_op jit(solution)/shard_map/pallas_call | solution.py:257
  243.9 0.0 copy-start
  243.9 0.0 copy-start.1
  243.9 4.6 all-to-all-start.1
  248.5 0.0 copy-done
  248.5 0.1 copy.10
  248.6 0.0 copy-done.1
  248.6 0.1 copy.11
  248.8 0.7 slice_bitcast_fusion.2
  249.4 92.4 %all-to-all-done.1 = bf16[16,8,64,256]{3,2,1,0:T(8,128)(2,1)} async-done(((bf16[16,8,64,256]{3,2,1,0:T(8,128)(2,1)}), bf16[16,8,64,256]{3,2,1,0:T(8,128)(2,1)}, u32[]{:S(2)}, u32[]{:S(2)}) %all-to-all-start.1) | async-done | bytes 4194336 | tf_op jit(solution)/shard_map/all_to_all | solution.py:271
  341.8 56.9 %shard_map.75 = (f32[64,128,256]{2,1,0:T(8,128)}, bf16[16,2,8,64,256]{4,3,2,1,0:T(8,128)(2,1)}) custom-call(s32[64]{0:T(128)} %dynamic_slice.6.row_chain, bf16[128,64,256]{2,1,0:T(8,128)(2,1)} %bitcast.6.mixed_ref, bf16[64,256,128]{2,1,0:T(8,128)(2,1)} %pair_ref.3, s32[64,256]{1,0:T(8,128)} %mask_ref.3, s32[1,256]{1,0:T(1,128)} %bitcast.34, ...), custom_call_target="tpu_custom_call" | custom-call | tf_op jit(solution)/shard_map/pallas_call | solution.py:178
  398.7 187.5 %all_to_all.21 = bf16[16,2,8,64,256]{4,3,2,1,0:T(8,128)(2,1)} all-to-all(bf16[16,2,8,64,256]{4,3,2,1,0:T(8,128)(2,1)} %get-tuple-element.7), channel_id=1, replica_groups=mesh['grp'=2,'row'=8,'chan'=2] {'row','chan'}, dimensions={0} | all-to-all | bytes 16777216 | tf_op jit(solution)/shard_map/all_to_all | solution.py:271
  586.2 9.0 %shard_map.76 = bf16[8,2,8,64,256]{4,3,2,1,0:T(8,128)(2,1)} custom-call(bf16[8,2,2,8,64,256]{5,4,3,2,1,0:T(8,128)(2,1)} %bitcast.24), custom_call_target="tpu_custom_call" | custom-call | tf_op jit(solution)/shard_map/pallas_call | solution.py:257
  595.2 97.7 %all_to_all.22 = bf16[16,8,64,256]{3,2,1,0:T(8,128)(2,1)} all-to-all(bf16[16,8,64,256]{3,2,1,0:T(8,128)(2,1)} %bitcast.26), channel_id=1, replica_groups=mesh['grp'=2,'row'=8,'chan'=2] {'row','chan'}, dimensions={0} | all-to-all | bytes 8388608 | tf_op jit(solution)/shard_map/all_to_all | solution.py:271
  692.9 26.8 %shard_map.77 = bf16[64,256,128]{2,1,0:T(8,128)(2,1)} custom-call(bf16[128,64,256]{2,1,0:T(8,128)(2,1)} %bitcast.27, f32[64,128,256]{2,1,0:T(8,128)} %get-tuple-element.8.state_ref, bf16[128,128]{1,0:T(8,128)(2,1)} %get-tuple-element.16.gate_ref, bf16[128,128]{1,0:T(8,128)(2,1)} %get-tuple-element.11.back_ref), custom_call_target="tpu_custom_call" | custom-call | tf_op jit(solution)/shard_map/pallas_call | solution.py:209
Async XLA Ops:
  243.9 4.6 copy-start
  243.9 4.7 copy-start.1
  243.9 97.9 %all-to-all-start.1 = ((bf16[16,8,64,256]{3,2,1,0:T(8,128)(2,1)}), bf16[16,8,64,256]{3,2,1,0:T(8,128)(2,1)}, u32[]{:S(2)}, u32[]{:S(2)}) async-start(bf16[16,8,64,256]{3,2,1,0:T(8,128)(2,1)} %bitcast.25), calls=%async_computation.1 | async-start | bytes 8388608 | tf_op jit(solution)/shard_map/all_to_all | solution.py:271

commit v2 on v1

--- a/solution.py
+++ b/solution.py
@@ -28,10 +28,8 @@
     return jnp.dot(a, b, preferred_element_type=jnp.float32)
 
 
-def first_state(pair_ref, same_row, embed_ref, eye_ref, i):
-    turned = lax.dot_general(
-        eye_ref[...], pair_ref[i], (((1,), (1,)), ((), ())), preferred_element_type=jnp.float32
-    )
+def first_state(pair_ref, same_row, embed_ref, i):
+    turned = pair_ref[i].astype(jnp.float32).T
     return turned + jnp.where(same_row, embed_ref[:, 1:2], embed_ref[:, 0:1])
 
 
@@ -77,15 +75,15 @@
 
 
 def start_kernel(
-    row_chain, pair_ref, mask_ref, col_chain, embed_ref, eye_ref, proj_ref, out_ref, left_scr, right_scr
+    row_chain, pair_ref, mask_ref, col_chain, embed_ref, proj_ref, out_ref, left_scr, right_scr
 ):
     rows = pair_ref.shape[0]
     step = pl.program_id(0)
 
-    @pl.loop(0, rows)
+    @pl.loop(0, rows, unroll=4)
     def _(i):
         same = col_chain[...] == row_chain[step * rows + i]
-        state = first_state(pair_ref, same, embed_ref, eye_ref, i)
+        state = first_state(pair_ref, same, embed_ref, i)
         normed = norm_channels(state).astype(jnp.bfloat16)
         mask_row = mask_ref[pl.ds(i, 1), :].astype(jnp.float32)
         project_row(normed, mask_row, proj_ref, left_scr, right_scr, i, rows)
@@ -94,7 +92,7 @@
 
 
 def middle_kernel(
-    row_chain, mixed_ref, pair_ref, mask_ref, col_chain, embed_ref, eye_ref, gate_ref, back_ref, proj_ref,
+    row_chain, mixed_ref, pair_ref, mask_ref, col_chain, embed_ref, gate_ref, back_ref, proj_ref,
     state_ref, out_ref, mixed_scr, left_scr, right_scr,
 ):
     rows = pair_ref.shape[0]
@@ -102,10 +100,10 @@
     step = pl.program_id(0)
     read_mixed(mixed_ref, mixed_scr)
 
-    @pl.loop(0, rows)
+    @pl.loop(0, rows, unroll=4)
     def _(i):
         same = col_chain[...] == row_chain[step * rows + i]
-        state = first_state(pair_ref, same, embed_ref, eye_ref, i)
+        state = first_state(pair_ref, same, embed_ref, i)
         normed = norm_channels(state).astype(jnp.bfloat16)
         gate = sigmoid(dot(gate_ref[...], normed))
         mixnorm = norm_channels(get_row(mixed_scr, i, rows, channels)).astype(jnp.bfloat16)
@@ -123,7 +121,7 @@
     channels = mixed_ref.shape[0]
     read_mixed(mixed_ref, mixed_scr)
 
-    @pl.loop(0, rows)
+    @pl.loop(0, rows, unroll=4)
     def _(i):
         state = state_ref[i]
         normed = norm_channels(state).astype(jnp.bfloat16)
@@ -148,7 +146,7 @@
 SMEM_SPEC = pl.BlockSpec(memory_space=pltpu.SMEM)
 
 
-def start_call(row_chain, pair, mask, col_chain, embed, eye, proj, targets, block):
+def start_call(row_chain, pair, mask, col_chain, embed, proj, targets, block):
     rows, cols, width = pair.shape
     hidden = proj.shape[0] // 4
     share = hidden // targets
@@ -161,17 +159,16 @@
             pl.BlockSpec((block, cols), lambda s: (s, 0)),
             whole(col_chain),
             whole(embed),
-            whole(eye),
             whole(proj),
         ],
         out_specs=pl.BlockSpec((targets, 2, share, block, cols), lambda s: (0, 0, 0, s, 0)),
         out_shape=jax.ShapeDtypeStruct((targets, 2, share, rows, cols), jnp.bfloat16),
         scratch_shapes=scratches(2, hidden, block, cols),
         compiler_params=params(),
-    )(row_chain, pair, mask, col_chain, embed, eye, proj)
-
-
-def middle_call(row_chain, mixed, pair, mask, col_chain, embed, eye, gate, back, proj, targets, block):
+    )(row_chain, pair, mask, col_chain, embed, proj)
+
+
+def middle_call(row_chain, mixed, pair, mask, col_chain, embed, gate, back, proj, targets, block):
     rows, cols, width = pair.shape
     hidden = proj.shape[0] // 4
     share = hidden // targets
@@ -185,7 +182,6 @@
             pl.BlockSpec((block, cols), lambda s: (s, 0)),
             whole(col_chain),
             whole(embed),
-            whole(eye),
             whole(gate),
             whole(back),
             whole(proj),
@@ -200,7 +196,7 @@
         ],
         scratch_shapes=scratches(3, hidden, block, cols),
         compiler_params=params(),
-    )(row_chain, mixed, pair, mask, col_chain, embed, eye, gate, back, proj)
+    )(row_chain, mixed, pair, mask, col_chain, embed, gate, back, proj)
 
 
 def end_call(mixed, state, gate, back, block):
@@ -280,15 +276,14 @@
     row_chain = lax.dynamic_slice_in_dim(chain_ids, lax.axis_index("row") * rows, rows)
     col_chain = lax.dynamic_slice_in_dim(chain_ids, lax.axis_index("chan") * cols, cols)[None, :]
     embed = chain_embed.T
-    eye = jnp.eye(width, dtype=jnp.bfloat16)
     proj, gate, back = (
         jnp.swapaxes(weight, 1, 2) for weight in (proj_weights, gate_weights, out_weights)
     )
 
-    sides = start_call(row_chain, pair, pair_mask, col_chain, embed, eye, proj[0], targets, block)
+    sides = start_call(row_chain, pair, pair_mask, col_chain, embed, proj[0], targets, block)
     mixed = exchange(product_call(exchange(sides), 0, row_parts, col_parts))
     state, sides = middle_call(
-        row_chain, mixed.reshape(hidden, rows, cols), pair, pair_mask, col_chain, embed, eye,
+        row_chain, mixed.reshape(hidden, rows, cols), pair, pair_mask, col_chain, embed,
         gate[0], back[0], proj[1], targets, block,
     )
     mixed = exchange(product_call(exchange(sides), 1, row_parts, col_parts))

time: 721 us -> 664 us (0.921)
  Pallas kernels: 140 us -> 83.9 us
    pallas_call x1, Pallas kernels: 56.9 us -> 32.1 us  [middle_call(): pl.pallas_call(middle_kernel, grid=(rows // block,), in_specs=[SMEM_SPEC,...]
    pallas_call x1, Pallas kernels: 38.7 us -> 19.3 us  [start_call(): pl.pallas_call(start_kernel, grid=(rows // block,), in_specs=[SMEM_SPEC,...]
    pallas_call x1, Pallas kernels: 26.8 us -> 14.5 us  [end_call(): pl.pallas_call(end_kernel, grid=(rows // block,), in_specs=[pl.BlockSpec(...]
where the time goes in v2:
time: 664 us; the launch traced here: 663 us
  blocking collectives  475 us (72%)
  waiting for transfers between devices  92.4 us (14%)
  Pallas kernels  83.9 us (13%)
  local copies, waits for them, and re-layouts  6.8 us (1%)
    all_to_all x3, blocking collectives, exchange(): lax.all_to_all(array, ('row', 'chan'), split_axis=0, concat_axis=0, tiled...  475 us
    all_to_all x1, waiting for transfers between devices, exchange(): lax.all_to_all(array, ('row', 'chan'), split_axis=0, concat_axis=0, tiled...  92.4 us
    pallas_call x1, Pallas kernels, middle_call(): pl.pallas_call(middle_kernel, grid=(rows // block,), in_specs=[SMEM_SPEC,...  32.1 us
    pallas_call x1, Pallas kernels, start_call(): pl.pallas_call(start_kernel, grid=(rows // block,), in_specs=[SMEM_SPEC,...  19.3 us
    pallas_call x2, Pallas kernels, product_call(): pl.pallas_call(functools.partial(product_kernel, update), grid=(share,),...  18 us
    pallas_call x1, Pallas kernels, end_call(): pl.pallas_call(end_kernel, grid=(rows // block,), in_specs=[pl.BlockSpec(...  14.5 us
  transfers between devices with their start and end apart: 1, of which 1 were waited for; matrix products, arithmetic and copies ran while one was open for 0% of the time, Pallas kernels for 0%

profile of v2, /device:TPU:9, one launch (start us, length us, event | category | flops | bytes accessed | tf_op | source)
XLA Modules:
  0.0 662.6 jit_solution(704729852691847756)
XLA Ops:
  0.0 1.3 dynamic_slice.6.row_chain
  1.3 1.3 dynamic_slice.7
  2.7 1.4 copy.8
  4.1 1.1 copy.9
  5.2 0.7 slice_bitcast_fusion
  5.9 19.3 %shard_map.73 = bf16[16,2,8,64,256]{4,3,2,1,0:T(8,128)(2,1)} custom-call(s32[64]{0:T(128)} %dynamic_slice.6.row_chain, bf16[64,256,128]{2,1,0:T(8,128)(2,1)} %pair_ref.3, s32[64,256]{1,0:T(8,128)} %mask_ref.3, s32[1,256]{1,0:T(1,128)} %bitcast.33, f32[128,2]{1,0:T(8,128)} %bitcast.29, bf16[512,128]{1,0:T(8,128)(2,1)} %get-tuple-element.10.proj_ref), custom_call_target="tpu_custom_call" | custom-call | tf_op jit(solution)/shard_map/pallas_call | solution.py:153
  25.2 189.7 %all_to_all.20 = bf16[16,2,8,64,256]{4,3,2,1,0:T(8,128)(2,1)} all-to-all(bf16[16,2,8,64,256]{4,3,2,1,0:T(8,128)(2,1)} %shard_map.73), channel_id=1, replica_groups=mesh['grp'=2,'row'=8,'chan'=2] {'row','chan'}, dimensions={0} | all-to-all | bytes 16777216 | tf_op jit(solution)/shard_map/all_to_all | solution.py:267
  214.9 9.0 %shard_map.74 = bf16[8,2,8,64,256]{4,3,2,1,0:T(8,128)(2,1)} custom-call(bf16[8,2,2,8,64,256]{5,4,3,2,1,0:T(8,128)(2,1)} %bitcast.23), custom_call_target="tpu_custom_call" | custom-call | tf_op jit(solution)/shard_map/pallas_call | solution.py:253
  223.9 0.0 copy-start
  223.9 0.0 copy-start.1
  223.9 4.6 all-to-all-start.1
  228.5 0.0 copy-done
  228.5 0.1 copy.10
  228.6 0.0 copy-done.1
  228.6 0.1 copy.11
  228.7 0.7 slice_bitcast_fusion.2
  229.4 92.4 %all-to-all-done.1 = bf16[16,8,64,256]{3,2,1,0:T(8,128)(2,1)} async-done(((bf16[16,8,64,256]{3,2,1,0:T(8,128)(2,1)}), bf16[16,8,64,256]{3,2,1,0:T(8,128)(2,1)}, u32[]{:S(2)}, u32[]{:S(2)}) %all-to-all-start.1) | async-done | bytes 4194336 | tf_op jit(solution)/shard_map/all_to_all | solution.py:267
  321.8 32.1 %shard_map.75 = (f32[64,128,256]{2,1,0:T(8,128)}, bf16[16,2,8,64,256]{4,3,2,1,0:T(8,128)(2,1)}) custom-call(s32[64]{0:T(128)} %dynamic_slice.6.row_chain, bf16[128,64,256]{2,1,0:T(8,128)(2,1)} %bitcast.6.mixed_ref, bf16[64,256,128]{2,1,0:T(8,128)(2,1)} %pair_ref.3, s32[64,256]{1,0:T(8,128)} %mask_ref.3, s32[1,256]{1,0:T(1,128)} %bitcast.34, ...), custom_call_target="tpu_custom_call" | custom-call | tf_op jit(solution)/shard_map/pallas_call | solution.py:175
  353.9 187.5 %all_to_all.21 = bf16[16,2,8,64,256]{4,3,2,1,0:T(8,128)(2,1)} all-to-all(bf16[16,2,8,64,256]{4,3,2,1,0:T(8,128)(2,1)} %get-tuple-element.7), channel_id=1, replica_groups=mesh['grp'=2,'row'=8,'chan'=2] {'row','chan'}, dimensions={0} | all-to-all | bytes 16777216 | tf_op jit(solution)/shard_map/all_to_all | solution.py:267
  541.4 9.0 %shard_map.76 = bf16[8,2,8,64,256]{4,3,2,1,0:T(8,128)(2,1)} custom-call(bf16[8,2,2,8,64,256]{5,4,3,2,1,0:T(8,128)(2,1)} %bitcast.24), custom_call_target="tpu_custom_call" | custom-call | tf_op jit(solution)/shard_map/pallas_call | solution.py:253
  550.4 97.7 %all_to_all.22 = bf16[16,8,64,256]{3,2,1,0:T(8,128)(2,1)} all-to-all(bf16[16,8,64,256]{3,2,1,0:T(8,128)(2,1)} %bitcast.26), channel_id=1, replica_groups=mesh['grp'=2,'row'=8,'chan'=2] {'row','chan'}, dimensions={0} | all-to-all | bytes 8388608 | tf_op jit(solution)/shard_map/all_to_all | solution.py:267
  648.1 14.5 %shard_map.77 = bf16[64,256,128]{2,1,0:T(8,128)(2,1)} custom-call(bf16[128,64,256]{2,1,0:T(8,128)(2,1)} %bitcast.27, f32[64,128,256]{2,1,0:T(8,128)} %get-tuple-element.8.state_ref, bf16[128,128]{1,0:T(8,128)(2,1)} %get-tuple-element.16.gate_ref, bf16[128,128]{1,0:T(8,128)(2,1)} %get-tuple-element.11.back_ref), custom_call_target="tpu_custom_call" | custom-call | tf_op jit(solution)/shard_map/pallas_call | solution.py:205
Async XLA Ops:
  223.9 4.6 copy-start
  223.9 4.7 copy-start.1
  223.9 97.9 %all-to-all-start.1 = ((bf16[16,8,64,256]{3,2,1,0:T(8,128)(2,1)}), bf16[16,8,64,256]{3,2,1,0:T(8,128)(2,1)}, u32[]{:S(2)}, u32[]{:S(2)}) async-start(bf16[16,8,64,256]{3,2,1,0:T(8,128)(2,1)} %bitcast.25), calls=%async_computation.1 | async-start | bytes 8388608 | tf_op jit(solution)/shard_map/all_to_all | solution.py:267

commit v3 on v2

v3 whole, which is shorter than its diff:
```python
import functools

import jax
import jax.numpy as jnp
from jax import lax
from jax.experimental import pallas as pl
from jax.experimental.pallas import tpu as pltpu
from jax.sharding import PartitionSpec as P

EPS = 1e-05
LANES = 128
VMEM = 56 * 1024 * 1024
FIRST, MIDDLE, LAST = (4, 12), (4, 12), (12, 4)


def sigmoid(x):
    return 0.5 * jnp.tanh(0.5 * x) + 0.5


def norm_channels(values):
    scale = 1.0 / values.shape[0]
    mean = jnp.sum(values, axis=0, keepdims=True) * scale
    centred = values - mean
    variance = jnp.sum(centred * centred, axis=0, keepdims=True) * scale
    return centred * lax.rsqrt(variance + EPS)


def dot(a, b):
    return jnp.dot(a, b, preferred_element_type=jnp.float32)


def same_chain(chains, chain_row, cols, rows, i):
    start = pl.multiple_of(lax.axis_index("chan") * cols, cols)
    return chain_row[:, pl.ds(start, cols)] == chains[lax.axis_index("row") * rows + i]


def first_state(pair_ref, same_row, embed_ref, i):
    turned = pair_ref[i].astype(jnp.float32).T
    return turned + jnp.where(same_row, embed_ref[:, 1:2], embed_ref[:, 0:1])


def put_row(scratch, i, rows, values):
    for part in range(values.shape[1] // LANES):
        scratch[part, pl.ds(i, values.shape[0], stride=rows), :] = values[
            :, part * LANES : (part + 1) * LANES
        ]


def get_row(scratch, i, rows, channels):
    return jnp.concatenate(
        [scratch[part, pl.ds(i, channels, stride=rows), :] for part in range(scratch.shape[0])],
        axis=1,
    )


def project_row(normed, mask_row, weight_ref, left_scr, right_scr, i, rows):
    hidden = weight_ref.shape[0] // 4
    proj = dot(weight_ref[...], normed)
    put_row(left_scr, i, rows, sigmoid(proj[:hidden]) * proj[hidden : 2 * hidden] * mask_row)
    put_row(
        right_scr, i, rows, sigmoid(proj[2 * hidden : 3 * hidden]) * proj[3 * hidden :] * mask_row
    )


def write_sides(left_scr, right_scr, out_ref):
    targets, _, share, rows, cols = out_ref.shape
    for side, scratch in enumerate((left_scr, right_scr)):
        for part in range(cols // LANES):
            out_ref[:, side, :, :, part * LANES : (part + 1) * LANES] = (
                scratch[part].astype(jnp.bfloat16).reshape(targets, share, rows, LANES)
            )


def read_mixed(mixed_ref, scratch):
    for part in range(scratch.shape[0]):
        scratch[part] = (
            mixed_ref[:, :, part * LANES : (part + 1) * LANES]
            .astype(jnp.float32)
            .reshape(scratch.shape[1:])
        )


def start_kernel(
    first, total_rows, row_chain, pair_ref, mask_ref, col_chain, embed_ref, proj_ref, out_ref, left_scr, right_scr
):
    rows = pair_ref.shape[0]
    step = pl.program_id(0) + first

    @pl.loop(0, rows, unroll=4)
    def _(i):
        same = same_chain(row_chain, col_chain, pair_ref.shape[1], total_rows, step * rows + i)
        state = first_state(pair_ref, same, embed_ref, i)
        normed = norm_channels(state).astype(jnp.bfloat16)
        mask_row = mask_ref[pl.ds(i, 1), :].astype(jnp.float32)
        project_row(normed, mask_row, proj_ref, left_scr, right_scr, i, rows)

    write_sides(left_scr, right_scr, out_ref)


def middle_kernel(
    first, total_rows, row_chain, mixed_ref, pair_ref, mask_ref, col_chain, embed_ref, gate_ref, back_ref, proj_ref,
    state_ref, out_ref, mixed_scr, left_scr, right_scr,
):
    rows = pair_ref.shape[0]
    channels = mixed_ref.shape[0]
    step = pl.program_id(0) + first
    read_mixed(mixed_ref, mixed_scr)

    @pl.loop(0, rows, unroll=4)
    def _(i):
        same = same_chain(row_chain, col_chain, pair_ref.shape[1], total_rows, step * rows + i)
        state = first_state(pair_ref, same, embed_ref, i)
        normed = norm_channels(state).astype(jnp.bfloat16)
        gate = sigmoid(dot(gate_ref[...], normed))
        mixnorm = norm_channels(get_row(mixed_scr, i, rows, channels)).astype(jnp.bfloat16)
        state = state + gate * dot(back_ref[...], mixnorm)
        state_ref[i] = state
        normed = norm_channels(state).astype(jnp.bfloat16)
        mask_row = mask_ref[pl.ds(i, 1), :].astype(jnp.float32)
        project_row(normed, mask_row, proj_ref, left_scr, right_scr, i, rows)

    write_sides(left_scr, right_scr, out_ref)


def end_kernel(mixed_ref, state_ref, gate_ref, back_ref, out_ref, mixed_scr):
    rows = state_ref.shape[0]
    channels = mixed_ref.shape[0]
    read_mixed(mixed_ref, mixed_scr)

    @pl.loop(0, rows, unroll=4)
    def _(i):
        state = state_ref[i]
        normed = norm_channels(state).astype(jnp.bfloat16)
        gate = sigmoid(dot(gate_ref[...], normed))
        mixnorm = norm_channels(get_row(mixed_scr, i, rows, channels)).astype(jnp.bfloat16)
        state = state + gate * dot(back_ref[...], mixnorm)
        out_ref[i] = state.T.astype(jnp.bfloat16)


def middle_kernel_onto(first, total_rows, *refs):
    middle_kernel(first, total_rows, *refs[:9], *refs[10:])


def end_kernel_onto(mixed_ref, state_ref, gate_ref, back_ref, earlier_ref, out_ref, mixed_scr):
    del earlier_ref
    end_kernel(mixed_ref, state_ref, gate_ref, back_ref, out_ref, mixed_scr)


def cost(pairs, multiplies, bytes_each):
    return pl.CostEstimate(
        flops=2 * pairs * multiplies, bytes_accessed=pairs * bytes_each, transcendentals=0
    )


def whole(array):
    return pl.BlockSpec(array.shape, lambda *_: (0,) * array.ndim)


def params():
    return pltpu.CompilerParams(vmem_limit_bytes=VMEM)


def scratches(count, channels, rows, cols):
    return [pltpu.VMEM((cols // LANES, channels * rows, LANES), jnp.float32)] * count


SMEM_SPEC = pl.BlockSpec(memory_space=pltpu.SMEM)


def start_call(row_chain, pair, mask, col_chain, embed, proj, targets, block, first, count):
    _, cols, width = pair.shape
    hidden = proj.shape[0] // 4
    share = hidden // targets
    return pl.pallas_call(
        functools.partial(start_kernel, first, pair.shape[0]),
        grid=(count,),
        in_specs=[
            SMEM_SPEC,
            pl.BlockSpec((block, cols, width), lambda s: (s + first, 0, 0)),
            pl.BlockSpec((block, cols), lambda s: (s + first, 0)),
            whole(col_chain),
            whole(embed),
            whole(proj),
        ],
        out_specs=pl.BlockSpec((targets, 2, share, block, cols), lambda s: (0, 0, 0, s, 0)),
        out_shape=jax.ShapeDtypeStruct((targets, 2, share, count * block, cols), jnp.bfloat16),
        scratch_shapes=scratches(2, hidden, block, cols),
        compiler_params=params(),
        cost_estimate=cost(count * block * cols, 5 * width * width, 4 * width),
    )(row_chain, pair, mask, col_chain, embed, proj)


def middle_call(
    row_chain, mixed, pair, mask, col_chain, embed, gate, back, proj, targets, block, first, count, earlier
):
    rows, cols, width = pair.shape
    hidden = proj.shape[0] // 4
    share = hidden // targets
    operands = [row_chain, mixed, pair, mask, col_chain, embed, gate, back, proj]
    in_specs = [
        SMEM_SPEC,
        pl.BlockSpec((hidden, block, cols), lambda s: (0, s, 0)),
        pl.BlockSpec((block, cols, width), lambda s: (s + first, 0, 0)),
        pl.BlockSpec((block, cols), lambda s: (s + first, 0)),
        whole(col_chain),
        whole(embed),
        whole(gate),
        whole(back),
        whole(proj),
    ]
    kernel, aliases = middle_kernel, {}
    if earlier is not None:
        kernel, aliases = middle_kernel_onto, {9: 0}
        operands.append(earlier)
        in_specs.append(pl.BlockSpec(memory_space=pl.ANY))
    return pl.pallas_call(
        functools.partial(kernel, first, rows),
        grid=(count,),
        in_specs=in_specs,
        out_specs=[
            pl.BlockSpec((block, width, cols), lambda s: (s + first, 0, 0)),
            pl.BlockSpec((targets, 2, share, block, cols), lambda s: (0, 0, 0, s, 0)),
        ],
        out_shape=[
            jax.ShapeDtypeStruct((rows, width, cols), jnp.float32),
            jax.ShapeDtypeStruct((targets, 2, share, count * block, cols), jnp.bfloat16),
        ],
        scratch_shapes=scratches(3, hidden, block, cols),
        input_output_aliases=aliases,
        compiler_params=params(),
        cost_estimate=cost(count * block * cols, 8 * width * width, 12 * width),
    )(*operands)


def end_call(mixed, state, gate, back, block, first, count, rows, earlier):
    _, width, cols = state.shape
    hidden = mixed.shape[0]
    kernel = end_kernel
    operands = [mixed, state, gate, back]
    in_specs = [
        pl.BlockSpec((hidden, block, cols), lambda s: (0, s, 0)),
        pl.BlockSpec((block, width, cols), lambda s: (s + first, 0, 0)),
        whole(gate),
        whole(back),
    ]
    aliases = {}
    if earlier is not None:
        kernel = end_kernel_onto
        operands.append(earlier)
        in_specs.append(pl.BlockSpec(memory_space=pl.ANY))
        aliases = {4: 0}
    return pl.pallas_call(
        kernel,
        grid=(count,),
        in_specs=in_specs,
        out_specs=pl.BlockSpec((block, cols, width), lambda s: (s + first, 0, 0)),
        out_shape=jax.ShapeDtypeStruct((rows, cols, width), jnp.bfloat16),
        scratch_shapes=scratches(1, hidden, block, cols),
        input_output_aliases=aliases,
        compiler_params=params(),
        cost_estimate=cost(count * block * cols, 2 * width * width, 8 * width),
    )(*operands)


def product_kernel(update, lefts, rights, wanted, *refs):
    left_refs, right_refs, outs = refs[:lefts], refs[lefts : lefts + rights], refs[lefts + rights :]
    row_parts, col_parts = right_refs[0].shape[:2]
    cols = right_refs[0].shape[-1]

    def side(held, part):
        held = [ref[:, part, 0, 0] for ref in held]
        return held[0] if len(held) == 1 else jnp.concatenate(held, axis=1)

    if update == 0:
        right = [side(right_refs, part).reshape(-1, cols) for part in range(col_parts)]
        for (first, count), out in zip(wanted, outs, strict=True):
            total = None
            for part in range(col_parts):
                left = side(left_refs, part)[:, first : first + count].reshape(-1, cols)
                term = lax.dot_general(
                    left, right[part], (((1,), (1,)), ((), ())), preferred_element_type=jnp.float32
                )
                total = term if total is None else total + term
            mixed = total.astype(jnp.bfloat16).reshape(row_parts, count, -1)
            for part in range(col_parts):
                out[:, part, 0] = mixed[:, :, part * cols : (part + 1) * cols]
    else:
        left = jnp.concatenate(
            [side(left_refs, part).reshape(-1, cols) for part in range(col_parts)], axis=1
        )
        for part in range(col_parts):
            mixed = lax.dot_general(
                left, side(right_refs, part).reshape(-1, cols), (((0,), (0,)), ((), ())),
                preferred_element_type=jnp.float32,
            ).astype(jnp.bfloat16)
            mixed = mixed.reshape(row_parts, -1, cols)
            for (first, count), out in zip(wanted, outs, strict=True):
                out[:, part, 0] = mixed[:, first : first + count]


def product_call(sides, update, row_parts, col_parts, wanted):
    targets, _, share, _, cols = sides[0].shape
    sides = [side.reshape(row_parts, col_parts, 2, share, -1, cols) for side in sides]
    size = row_parts * sum(side.shape[4] for side in sides)
    lefts, shift = sides, 0
    if update == 0:
        lefts, start = [], 0
        first, last = wanted[0][0], wanted[-1][0] + wanted[-1][1]
        for side in sides:
            end = start + side.shape[4]
            if end <= first:
                shift = end
            elif start < last:
                lefts.append(side)
            start = end
    wanted = [(first - shift, count) for first, count in wanted]

    def spec(side, which):
        return pl.BlockSpec(
            (row_parts, col_parts, 1, 1, side.shape[4], cols), lambda s: (0, 0, which, s, 0, 0)
        )

    outs = pl.pallas_call(
        functools.partial(product_kernel, update, len(lefts), len(sides), wanted),
        grid=(share,),
        in_specs=[spec(side, 0) for side in lefts] + [spec(side, 1) for side in sides],
        out_specs=[
            pl.BlockSpec((row_parts, col_parts, 1, count, cols), lambda s: (0, 0, s, 0, 0))
            for _, count in wanted
        ],
        out_shape=[
            jax.ShapeDtypeStruct((row_parts, col_parts, share, count, cols), jnp.bfloat16)
            for _, count in wanted
        ],
        compiler_params=params(),
        cost_estimate=cost(share * size * size, size, 6),
    )(*lefts, *sides)
    return [out.reshape(targets, share, -1, cols) for out in outs]


def exchange(array):
    return lax.all_to_all(array, ("row", "chan"), split_axis=0, concat_axis=0, tiled=True)


def local(mesh, pair, pair_mask, chain_ids, chain_embed, proj_weights, gate_weights, out_weights):
    rows, cols, width = pair.shape
    row_parts, col_parts = mesh.shape["row"], mesh.shape["chan"]
    targets = row_parts * col_parts
    hidden = out_weights.shape[1]
    block = 16
    row_chain, col_chain = chain_ids, chain_ids[None, :]
    embed = chain_embed.T
    proj, gate, back = (
        jnp.swapaxes(weight, 1, 2) for weight in (proj_weights, gate_weights, out_weights)
    )

    def pieces(sixteenths):
        blocks, spans, start = rows // block, [], 0
        for part in sixteenths:
            count = blocks * part // 16
            spans.append((start, count))
            start += count
        return spans

    def rows_of(spans):
        return [(first * block, count * block) for first, count in spans]

    sides = [
        exchange(
            start_call(
                row_chain, pair, pair_mask, col_chain, embed, proj[0], targets, block, first, count
            )
        )
        for first, count in pieces(FIRST)
    ]
    mixed = []
    for span in rows_of(pieces(MIDDLE)):
        mixed += [exchange(part) for part in product_call(sides, 0, row_parts, col_parts, [span])]
    state, sides = None, []
    for (first, count), part in zip(pieces(MIDDLE), mixed, strict=True):
        state, part = middle_call(
            row_chain, part.reshape(hidden, -1, cols), pair, pair_mask, col_chain, embed,
            gate[0], back[0], proj[1], targets, block, first, count, state,
        )
        sides.append(exchange(part))
    mixed = [
        exchange(part)
        for part in product_call(sides, 1, row_parts, col_parts, rows_of(pieces(LAST)))
    ]
    updated = None
    for (first, count), part in zip(pieces(LAST), mixed, strict=True):
        updated = end_call(
            part.reshape(hidden, -1, cols), state, gate[1], back[1], block, first, count, rows, updated
        )
    return updated


def solution(mesh):
    placed = (
        P(("grp", "row"), "chan", None),
        P(("grp", "row"), "chan"),
        P("grp"),
        P(),
        P(),
        P(),
        P(),
    )
    return jax.shard_map(
        functools.partial(local, mesh),
        mesh=mesh,
        in_specs=placed,
        out_specs=P(("grp", "row"), "chan", None),
        check_vma=False,
    )
```

time: 664 us -> 639 us (0.962)
  blocking collectives: 475 us -> 360 us
  waiting for transfers between devices: 92.4 us -> 148 us
  starting transfers between devices: 4.57 us -> 23.2 us
  Pallas kernels: 83.9 us -> 98.8 us
    all_to_all x3, blocking collectives: 475 us -> 360 us  [exchange(): lax.all_to_all(array, ('row', 'chan'), split_axis=0, concat_axis=0, tiled...]
    all_to_all x1 -> x5, waiting for transfers between devices: 92.4 us -> 148 us  [exchange(): lax.all_to_all(array, ('row', 'chan'), split_axis=0, concat_axis=0, tiled...]
    all_to_all x1 -> x5, starting transfers between devices: 4.57 us -> 23.2 us  [exchange(): lax.all_to_all(array, ('row', 'chan'), split_axis=0, concat_axis=0, tiled...]
    pallas_call x5 -> x9, Pallas kernels: 83.9 us -> 98.8 us  [the longest x2 35 us: middle_call(): pl.pallas_call(functools.partial(kernel, first, rows), grid=(count,), in_...]
  transfers between devices with their start and end apart: 1 -> 5, of which waited for: 1 -> 5; matrix products, arithmetic and copies ran while one was open for 0% -> 0% of each run, Pallas kernels for 0% -> 11%
where the time goes in v3:
time: 639 us; the launch traced here: 638 us
  blocking collectives  360 us (56%)
  waiting for transfers between devices  148 us (23%)
  Pallas kernels  98.8 us (15%)
  starting transfers between devices  23.2 us (4%)
  local copies, waits for them, and re-layouts  7.96 us (1%)
    all_to_all x3, blocking collectives, exchange(): lax.all_to_all(array, ('row', 'chan'), split_axis=0, concat_axis=0, tiled...  360 us
    all_to_all x5, waiting for transfers between devices, exchange(): lax.all_to_all(array, ('row', 'chan'), split_axis=0, concat_axis=0, tiled...  148 us
    pallas_call x2, Pallas kernels, middle_call(): pl.pallas_call(functools.partial(kernel, first, rows), grid=(count,), in_...  35 us
    pallas_call x3, Pallas kernels, product_call(): pl.pallas_call(functools.partial(product_kernel, update, len(lefts), len(...  24.4 us
    all_to_all x5, starting transfers between devices, exchange(): lax.all_to_all(array, ('row', 'chan'), split_axis=0, concat_axis=0, tiled...  23.2 us
    pallas_call x2, Pallas kernels, start_call(): pl.pallas_call(functools.partial(start_kernel, first, pair.shape[0]), gri...  22 us
    pallas_call x2, Pallas kernels, end_call(): pl.pallas_call(kernel, grid=(count,), in_specs=in_specs, out_specs=pl.Blo...  17.3 us
  transfers between devices with their start and end apart: 5, of which 5 were waited for; matrix products, arithmetic and copies ran while one was open for 0% of the time, Pallas kernels for 11%

profile of v3, /device:TPU:9, one launch (start us, length us, event | category | flops | bytes accessed | tf_op | source)
XLA Modules:
  0.0 637.9 jit_solution(937993018442524035)
XLA Ops:
  0.0 1.4 copy.10
  1.4 1.1 copy.11
  2.5 0.7 slice_bitcast_fusion
  3.2 6.8 %shard_map.73 = bf16[16,2,8,16,256]{4,3,2,1,0:T(8,128)(2,1)} custom-call(s32[512]{0:T(512)} %refs_0_.1, bf16[64,256,128]{2,1,0:T(8,128)(2,1)} %refs_2_.1, s32[64,256]{1,0:T(8,128)} %refs_3_.1, s32[1,512]{1,0:T(1,128)} %bitcast.53, f32[128,2]{1,0:T(8,128)} %bitcast.46, bf16[512,128]{1,0:T(8,128)(2,1)} %get-tuple-element.18.proj_ref), custom_call_target="tpu_custom_call" | custom-call | flops 671088640 | bytes 2097152 | tf_op jit(solution)/shard_map/pallas_call | solution.py:174
  10.0 6.6 %all-to-all-start = ((bf16[16,2,8,16,256]{4,3,2,1,0:T(8,128)(2,1)}), bf16[16,2,8,16,256]{4,3,2,1,0:T(8,128)(2,1)S(1)}, u32[]{:S(2)}, u32[]{:S(2)}) async-start(bf16[16,2,8,16,256]{4,3,2,1,0:T(8,128)(2,1)} %shard_map.73), calls=%async_computation | async-start | bytes 4194304 | tf_op jit(solution)/shard_map/all_to_all | solution.py:342
  16.6 15.3 %shard_map.74 = bf16[16,2,8,48,256]{4,3,2,1,0:T(8,128)(2,1)} custom-call(s32[512]{0:T(512)} %refs_0_.1, bf16[64,256,128]{2,1,0:T(8,128)(2,1)} %refs_2_.1, s32[64,256]{1,0:T(8,128)} %refs_3_.1, s32[1,512]{1,0:T(1,128)} %bitcast.54, f32[128,2]{1,0:T(8,128)} %bitcast.47, bf16[512,128]{1,0:T(8,128)(2,1)} %get-tuple-element.18.proj_ref), custom_call_target="tpu_custom_call" | custom-call | flops 2013265920 | bytes 6291456 | tf_op jit(solution)/shard_map/pallas_call | solution.py:174
  31.8 33.0 %all-to-all-done = bf16[16,2,8,16,256]{4,3,2,1,0:T(8,128)(2,1)S(1)} async-done(((bf16[16,2,8,16,256]{4,3,2,1,0:T(8,128)(2,1)}), bf16[16,2,8,16,256]{4,3,2,1,0:T(8,128)(2,1)S(1)}, u32[]{:S(2)}, u32[]{:S(2)}) %all-to-all-start) | async-done | bytes 2097184 | tf_op jit(solution)/shard_map/all_to_all | solution.py:342
  64.8 142.5 %all_to_all.40 = bf16[16,2,8,48,256]{4,3,2,1,0:T(8,128)(2,1)} all-to-all(bf16[16,2,8,48,256]{4,3,2,1,0:T(8,128)(2,1)} %shard_map.74), channel_id=1, replica_groups=mesh['grp'=2,'row'=8,'chan'=2] {'row','chan'}, dimensions={0} | all-to-all | bytes 12582912 | tf_op jit(solution)/shard_map/all_to_all | solution.py:342
  207.4 7.3 %shard_map.75 = bf16[8,2,8,16,256]{4,3,2,1,0:T(8,128)(2,1)} custom-call(bf16[8,2,2,8,16,256]{5,4,3,2,1,0:T(8,128)(2,1)} %bitcast.34, bf16[8,2,2,8,16,256]{5,4,3,2,1,0:T(8,128)(2,1)} %bitcast.35, bf16[8,2,2,8,48,256]{5,4,3,2,1,0:T(8,128)(2,1)} %bitcast.29), custom_call_target="tpu_custom_call" | custom-call | flops 2147483648 | bytes 12582912 | tf_op jit(solution)/shard_map/pallas_call | solution.py:323
  214.6 4.2 all-to-all-start.2
  218.8 8.3 %shard_map.77 = bf16[8,2,8,48,256]{4,3,2,1,0:T(8,128)(2,1)} custom-call(bf16[8,2,2,8,48,256]{5,4,3,2,1,0:T(8,128)(2,1)} %bitcast.30, bf16[8,2,2,8,16,256]{5,4,3,2,1,0:T(8,128)(2,1)} %bitcast.36, bf16[8,2,2,8,48,256]{5,4,3,2,1,0:T(8,128)(2,1)} %bitcast.31), custom_call_target="tpu_custom_call" | custom-call | flops 2147483648 | bytes 12582912 | tf_op jit(solution)/shard_map/pallas_call | solution.py:323
  227.1 17.5 %all-to-all-done.2 = bf16[16,8,16,256]{3,2,1,0:T(8,128)(2,1)S(1)} async-done(((bf16[16,8,16,256]{3,2,1,0:T(8,128)(2,1)}), bf16[16,8,16,256]{3,2,1,0:T(8,128)(2,1)S(1)}, u32[]{:S(2)}, u32[]{:S(2)}) %all-to-all-start.2) | async-done | bytes 1048608 | tf_op jit(solution)/shard_map/all_to_all | solution.py:342
  244.6 1.1 copy-done.4
  245.6 4.0 all-to-all-start.4
  249.6 0.0 copy-done.5
  249.6 0.1 copy.12
  249.7 0.1 copy.13
  249.9 0.7 slice_bitcast_fusion.2
  250.5 10.0 %shard_map.76 = (f32[64,128,256]{2,1,0:T(8,128)}, bf16[16,2,8,16,256]{4,3,2,1,0:T(8,128)(2,1)}) custom-call(s32[512]{0:T(512)} %refs_0_.1, bf16[128,16,256]{2,1,0:T(8,128)(2,1)} %bitcast.43, bf16[64,256,128]{2,1,0:T(8,128)(2,1)} %refs_2_.1, s32[64,256]{1,0:T(8,128)} %refs_3_.1, s32[1,512]{1,0:T(1,128)} %bitcast.55, f32[128,2]{1,0:T(8,128)} %bitcast.48, ...), custom_call_target="tpu_custom_call" | custom-call | flops 1073741824 | bytes 6291456 | tf_op jit(solution)/shard_map/pallas_call | solution.py:216
  260.5 59.8 %all-to-all-done.4 = bf16[16,8,48,256]{3,2,1,0:T(8,128)(2,1)S(1)} async-done(((bf16[16,8,48,256]{3,2,1,0:T(8,128)(2,1)}), bf16[16,8,48,256]{3,2,1,0:T(8,128)(2,1)S(1)}, u32[]{:S(2)}, u32[]{:S(2)}) %all-to-all-start.4) | async-done | bytes 3145760 | tf_op jit(solution)/shard_map/all_to_all | solution.py:342
  320.3 1.7 copy-done.2
  322.0 4.4 all-to-all-start.3
  326.4 25.0 %shard_map.78 = (f32[64,128,256]{2,1,0:T(8,128)}, bf16[16,2,8,48,256]{4,3,2,1,0:T(8,128)(2,1)}) custom-call(s32[512]{0:T(512)} %refs_0_.1, bf16[128,48,256]{2,1,0:T(8,128)(2,1)} %bitcast.39, bf16[64,256,128]{2,1,0:T(8,128)(2,1)} %refs_2_.1, s32[64,256]{1,0:T(8,128)} %refs_3_.1, s32[1,512]{1,0:T(1,128)} %bitcast.56, ...), custom_call_target="tpu_custom_call", output_to_operand_aliasing={{0}: (9, {})} | custom-call | flops 3221225472 | bytes 18874368 | tf_op jit(solution)/shard_map/pallas_call | solution.py:216
  351.4 23.2 %all-to-all-done.3 = bf16[16,2,8,16,256]{4,3,2,1,0:T(8,128)(2,1)S(1)} async-done(((bf16[16,2,8,16,256]{4,3,2,1,0:T(8,128)(2,1)}), bf16[16,2,8,16,256]{4,3,2,1,0:T(8,128)(2,1)S(1)}, u32[]{:S(2)}, u32[]{:S(2)}) %all-to-all-start.3) | async-done | bytes 2097184 | tf_op jit(solution)/shard_map/all_to_all | solution.py:342
  374.6 142.5 %all_to_all.41 = bf16[16,2,8,48,256]{4,3,2,1,0:T(8,128)(2,1)} all-to-all(bf16[16,2,8,48,256]{4,3,2,1,0:T(8,128)(2,1)} %get-tuple-element.13), channel_id=1, replica_groups=mesh['grp'=2,'row'=8,'chan'=2] {'row','chan'}, dimensions={0} | all-to-all | bytes 12582912 | tf_op jit(solution)/shard_map/all_to_all | solution.py:342
  517.2 8.9 %shard_map.79 = (bf16[8,2,8,48,256]{4,3,2,1,0:T(8,128)(2,1)}, bf16[8,2,8,16,256]{4,3,2,1,0:T(8,128)(2,1)}) custom-call(bf16[8,2,2,8,16,256]{5,4,3,2,1,0:T(8,128)(2,1)} %bitcast.37, bf16[8,2,2,8,48,256]{5,4,3,2,1,0:T(8,128)(2,1)} %bitcast.32, bf16[8,2,2,8,16,256]{5,4,3,2,1,0:T(8,128)(2,1)} %bitcast.38, bf16[8,2,2,8,48,256]{5,4,3,2,1,0:T(8,128)(2,1)} %bitcast.33), custom_call_target="tpu_custom_call" | custom-call | flops 2147483648 | bytes 12582912 | tf_op jit(solution)/shard_map/pallas_call | solution.py:323
  526.1 75.2 %all_to_all.42 = bf16[16,8,48,256]{3,2,1,0:T(8,128)(2,1)} all-to-all(bf16[16,8,48,256]{3,2,1,0:T(8,128)(2,1)} %bitcast.45), channel_id=1, replica_groups=mesh['grp'=2,'row'=8,'chan'=2] {'row','chan'}, dimensions={0} | all-to-all | bytes 6291456 | tf_op jit(solution)/shard_map/all_to_all | solution.py:342
  601.3 4.1 all-to-all-start.6
  605.4 11.6 %shard_map.80.earlier_ref = bf16[64,256,128]{2,1,0:T(8,128)(2,1)} custom-call(bf16[128,48,256]{2,1,0:T(8,128)(2,1)} %bitcast.41, f32[64,128,256]{2,1,0:T(8,128)} %get-tuple-element.15.state_ref, bf16[128,128]{1,0:T(8,128)(2,1)} %get-tuple-element.24.gate_ref, bf16[128,128]{1,0:T(8,128)(2,1)} %get-tuple-element.19.back_ref), custom_call_target="tpu_custom_call" | custom-call | flops 805306368 | bytes 12582912 | tf_op jit(solution)/shard_map/pallas_call | solution.py:252
  617.0 14.1 %all-to-all-done.6 = bf16[16,8,16,256]{3,2,1,0:T(8,128)(2,1)S(1)} async-done(((bf16[16,8,16,256]{3,2,1,0:T(8,128)(2,1)}), bf16[16,8,16,256]{3,2,1,0:T(8,128)(2,1)S(1)}, u32[]{:S(2)}, u32[]{:S(2)}) %all-to-all-start.6) | async-done | bytes 1048608 | tf_op jit(solution)/shard_map/all_to_all | solution.py:342
  631.2 1.1 copy-done.3
  632.2 5.7 shard_map.81
  (10 shorter events, 0.0 us)
Async XLA Ops:
  10.0 54.8 %all-to-all-start = ((bf16[16,2,8,16,256]{4,3,2,1,0:T(8,128)(2,1)}), bf16[16,2,8,16,256]{4,3,2,1,0:T(8,128)(2,1)S(1)}, u32[]{:S(2)}, u32[]{:S(2)}) async-start(bf16[16,2,8,16,256]{4,3,2,1,0:T(8,128)(2,1)} %shard_map.73), calls=%async_computation | async-start | bytes 4194304 | tf_op jit(solution)/shard_map/all_to_all | solution.py:342
  64.8 142.5 %copy-start = (bf16[16,2,8,16,256]{4,3,2,1,0:T(8,128)(2,1)}, bf16[16,2,8,16,256]{4,3,2,1,0:T(8,128)(2,1)S(1)}, u32[]{:S(2)}) copy-start(bf16[16,2,8,16,256]{4,3,2,1,0:T(8,128)(2,1)S(1)} %all-to-all-done) | copy-start | bytes 6291460
  214.6 29.9 %all-to-all-start.2 = ((bf16[16,8,16,256]{3,2,1,0:T(8,128)(2,1)}), bf16[16,8,16,256]{3,2,1,0:T(8,128)(2,1)S(1)}, u32[]{:S(2)}, u32[]{:S(2)}) async-start(bf16[16,8,16,256]{3,2,1,0:T(8,128)(2,1)} %bitcast.44), calls=%async_computation.2 | async-start | bytes 2097152 | tf_op jit(solution)/shard_map/all_to_all | solution.py:342
  227.1 22.5 %copy-start.5 = (bf16[2,128,128]{2,1,0:T(8,128)(2,1)S(1)}, bf16[2,128,128]{2,1,0:T(8,128)(2,1)}, u32[]{:S(2)}) copy-start(bf16[2,128,128]{2,1,0:T(8,128)(2,1)} %param.12) | copy-start | bytes 196612
  227.1 22.6 %copy-start.6 = (bf16[2,128,128]{2,1,0:T(8,128)(2,1)S(1)}, bf16[2,128,128]{2,1,0:T(8,128)(2,1)}, u32[]{:S(2)}) copy-start(bf16[2,128,128]{2,1,0:T(8,128)(2,1)} %param.13) | copy-start | bytes 196612
  244.6 1.1 copy-start.4
  245.6 74.7 %all-to-all-start.4 = ((bf16[16,8,48,256]{3,2,1,0:T(8,128)(2,1)}), bf16[16,8,48,256]{3,2,1,0:T(8,128)(2,1)S(1)}, u32[]{:S(2)}, u32[]{:S(2)}) async-start(bf16[16,8,48,256]{3,2,1,0:T(8,128)(2,1)} %bitcast.40), calls=%async_computation.4 | async-start | bytes 6291456 | tf_op jit(solution)/shard_map/all_to_all | solution.py:342
  320.3 1.7 copy-start.2
  322.0 52.6 %all-to-all-start.3 = ((bf16[16,2,8,16,256]{4,3,2,1,0:T(8,128)(2,1)}), bf16[16,2,8,16,256]{4,3,2,1,0:T(8,128)(2,1)S(1)}, u32[]{:S(2)}, u32[]{:S(2)}) async-start(bf16[16,2,8,16,256]{4,3,2,1,0:T(8,128)(2,1)} %get-tuple-element.11), calls=%async_computation.3 | async-start | bytes 4194304 | tf_op jit(solution)/shard_map/all_to_all | solution.py:342
  374.6 142.5 %copy-start.1 = (bf16[16,2,8,16,256]{4,3,2,1,0:T(8,128)(2,1)}, bf16[16,2,8,16,256]{4,3,2,1,0:T(8,128)(2,1)S(1)}, u32[]{:S(2)}) copy-start(bf16[16,2,8,16,256]{4,3,2,1,0:T(8,128)(2,1)S(1)} %all-to-all-done.3) | copy-start | bytes 6291460
  601.3 29.9 %all-to-all-start.6 = ((bf16[16,8,16,256]{3,2,1,0:T(8,128)(2,1)}), bf16[16,8,16,256]{3,2,1,0:T(8,128)(2,1)S(1)}, u32[]{:S(2)}, u32[]{:S(2)}) async-start(bf16[16,8,16,256]{3,2,1,0:T(8,128)(2,1)} %bitcast.17), calls=%async_computation.6 | async-start | bytes 2097152 | tf_op jit(solution)/shard_map/all_to_all | solution.py:342
  631.2 1.1 copy-start.3

commit v4 on v3

--- a/solution.py
+++ b/solution.py
@@ -1,4 +1,5 @@
 import functools
+import math
 
 import jax
 import jax.numpy as jnp
@@ -9,7 +10,8 @@
 
 EPS = 1e-05
 LANES = 128
-VMEM = 56 * 1024 * 1024
+CHANNELS = 4
+VMEM = 60 * 1024 * 1024
 FIRST, MIDDLE, LAST = (4, 12), (4, 12), (12, 4)
 
 
@@ -34,9 +36,16 @@
     return chain_row[:, pl.ds(start, cols)] == chains[lax.axis_index("row") * rows + i]
 
 
-def first_state(pair_ref, same_row, embed_ref, i):
+def turn_embed(embed_ref, embed_scr):
+    _, width, cols = embed_scr.shape
+    for kind in range(2):
+        rows = jnp.broadcast_to(embed_ref[kind : kind + 1, :], (cols, width))
+        embed_scr[kind] = rows.T
+
+
+def first_state(pair_ref, same_row, embed_scr, i):
     turned = pair_ref[i].astype(jnp.float32).T
-    return turned + jnp.where(same_row, embed_ref[:, 1:2], embed_ref[:, 0:1])
+    return turned + jnp.where(same_row, embed_scr[1], embed_scr[0])
 
 
 def put_row(scratch, i, rows, values):
@@ -81,15 +90,16 @@
 
 
 def start_kernel(
-    first, total_rows, row_chain, pair_ref, mask_ref, col_chain, embed_ref, proj_ref, out_ref, left_scr, right_scr
+    first, total_rows, row_chain, pair_ref, mask_ref, col_chain, embed_ref, proj_ref, out_ref, left_scr, right_scr, embed_scr
 ):
     rows = pair_ref.shape[0]
     step = pl.program_id(0) + first
+    turn_embed(embed_ref, embed_scr)
 
     @pl.loop(0, rows, unroll=4)
     def _(i):
         same = same_chain(row_chain, col_chain, pair_ref.shape[1], total_rows, step * rows + i)
-        state = first_state(pair_ref, same, embed_ref, i)
+        state = first_state(pair_ref, same, embed_scr, i)
         normed = norm_channels(state).astype(jnp.bfloat16)
         mask_row = mask_ref[pl.ds(i, 1), :].astype(jnp.float32)
         project_row(normed, mask_row, proj_ref, left_scr, right_scr, i, rows)
@@ -99,17 +109,18 @@
 
 def middle_kernel(
     first, total_rows, row_chain, mixed_ref, pair_ref, mask_ref, col_chain, embed_ref, gate_ref, back_ref, proj_ref,
-    state_ref, out_ref, mixed_scr, left_scr, right_scr,
+    state_ref, out_ref, mixed_scr, left_scr, right_scr, embed_scr,
 ):
     rows = pair_ref.shape[0]
     channels = mixed_ref.shape[0]
     step = pl.program_id(0) + first
+    turn_embed(embed_ref, embed_scr)
     read_mixed(mixed_ref, mixed_scr)
 
     @pl.loop(0, rows, unroll=4)
     def _(i):
         same = same_chain(row_chain, col_chain, pair_ref.shape[1], total_rows, step * rows + i)
-        state = first_state(pair_ref, same, embed_ref, i)
+        state = first_state(pair_ref, same, embed_scr, i)
         normed = norm_channels(state).astype(jnp.bfloat16)
         gate = sigmoid(dot(gate_ref[...], normed))
         mixnorm = norm_channels(get_row(mixed_scr, i, rows, channels)).astype(jnp.bfloat16)
@@ -184,7 +195,7 @@
         ],
         out_specs=pl.BlockSpec((targets, 2, share, block, cols), lambda s: (0, 0, 0, s, 0)),
         out_shape=jax.ShapeDtypeStruct((targets, 2, share, count * block, cols), jnp.bfloat16),
-        scratch_shapes=scratches(2, hidden, block, cols),
+        scratch_shapes=scratches(2, hidden, block, cols) + [pltpu.VMEM((2, width, cols), jnp.float32)],
         compiler_params=params(),
         cost_estimate=cost(count * block * cols, 5 * width * width, 4 * width),
     )(row_chain, pair, mask, col_chain, embed, proj)
@@ -225,7 +236,7 @@
             jax.ShapeDtypeStruct((rows, width, cols), jnp.float32),
             jax.ShapeDtypeStruct((targets, 2, share, count * block, cols), jnp.bfloat16),
         ],
-        scratch_shapes=scratches(3, hidden, block, cols),
+        scratch_shapes=scratches(3, hidden, block, cols) + [pltpu.VMEM((2, width, cols), jnp.float32)],
         input_output_aliases=aliases,
         compiler_params=params(),
         cost_estimate=cost(count * block * cols, 8 * width * width, 12 * width),
@@ -263,12 +274,17 @@
 
 
 def product_kernel(update, lefts, rights, wanted, *refs):
+    for channel in range(refs[0].shape[3]):
+        product_channel(channel, update, lefts, rights, wanted, *refs)
+
+
+def product_channel(channel, update, lefts, rights, wanted, *refs):
     left_refs, right_refs, outs = refs[:lefts], refs[lefts : lefts + rights], refs[lefts + rights :]
     row_parts, col_parts = right_refs[0].shape[:2]
     cols = right_refs[0].shape[-1]
 
     def side(held, part):
-        held = [ref[:, part, 0, 0] for ref in held]
+        held = [ref[:, part, 0, channel] for ref in held]
         return held[0] if len(held) == 1 else jnp.concatenate(held, axis=1)
 
     if update == 0:
@@ -283,7 +299,7 @@
                 total = term if total is None else total + term
             mixed = total.astype(jnp.bfloat16).reshape(row_parts, count, -1)
             for part in range(col_parts):
-                out[:, part, 0] = mixed[:, :, part * cols : (part + 1) * cols]
+                out[:, part, channel] = mixed[:, :, part * cols : (part + 1) * cols]
     else:
         left = jnp.concatenate(
             [side(left_refs, part).reshape(-1, cols) for part in range(col_parts)], axis=1
@@ -295,7 +311,7 @@
             ).astype(jnp.bfloat16)
             mixed = mixed.reshape(row_parts, -1, cols)
             for (first, count), out in zip(wanted, outs, strict=True):
-                out[:, part, 0] = mixed[:, first : first + count]
+                out[:, part, channel] = mixed[:, first : first + count]
 
 
 def product_call(sides, update, row_parts, col_parts, wanted):
@@ -314,18 +330,19 @@
                 lefts.append(side)
             start = end
     wanted = [(first - shift, count) for first, count in wanted]
+    step = math.gcd(share, CHANNELS)
 
     def spec(side, which):
         return pl.BlockSpec(
-            (row_parts, col_parts, 1, 1, side.shape[4], cols), lambda s: (0, 0, which, s, 0, 0)
+            (row_parts, col_parts, 1, step, side.shape[4], cols), lambda s: (0, 0, which, s, 0, 0)
         )
 
     outs = pl.pallas_call(
         functools.partial(product_kernel, update, len(lefts), len(sides), wanted),
-        grid=(share,),
+        grid=(share // step,),
         in_specs=[spec(side, 0) for side in lefts] + [spec(side, 1) for side in sides],
         out_specs=[
-            pl.BlockSpec((row_parts, col_parts, 1, count, cols), lambda s: (0, 0, s, 0, 0))
+            pl.BlockSpec((row_parts, col_parts, step, count, cols), lambda s: (0, 0, s, 0, 0))
             for _, count in wanted
         ],
         out_shape=[
@@ -349,7 +366,7 @@
     hidden = out_weights.shape[1]
     block = 16
     row_chain, col_chain = chain_ids, chain_ids[None, :]
-    embed = chain_embed.T
+    embed = chain_embed
     proj, gate, back = (
         jnp.swapaxes(weight, 1, 2) for weight in (proj_weights, gate_weights, out_weights)
     )

time: 639 us -> 631 us (0.987)
  Pallas kernels: 98.8 us -> 88.8 us
    pallas_call x3, Pallas kernels: 24.4 us -> 15.7 us  [product_call(): pl.pallas_call(functools.partial(product_kernel, update, len(lefts), len(...]
  transfers between devices with their start and end apart: 5 -> 5, of which waited for: 5 -> 5; matrix products, arithmetic and copies ran while one was open for 0% -> 0% of each run, Pallas kernels for 11% -> 10%
where the time goes in v4:
time: 631 us
  blocking collectives  360 us (57%)
  waiting for transfers between devices  152 us (24%)
  Pallas kernels  88.8 us (14%)
  starting transfers between devices  23.2 us (4%)
  local copies, waits for them, and re-layouts  6.56 us (1%)
    all_to_all x3, blocking collectives, exchange(): lax.all_to_all(array, ('row', 'chan'), split_axis=0, concat_axis=0, tiled...  360 us
    all_to_all x5, waiting for transfers between devices, exchange(): lax.all_to_all(array, ('row', 'chan'), split_axis=0, concat_axis=0, tiled...  152 us
    pallas_call x2, Pallas kernels, middle_call(): pl.pallas_call(functools.partial(kernel, first, rows), grid=(count,), in_...  34.1 us
    all_to_all x5, starting transfers between devices, exchange(): lax.all_to_all(array, ('row', 'chan'), split_axis=0, concat_axis=0, tiled...  23.2 us
    pallas_call x2, Pallas kernels, start_call(): pl.pallas_call(functools.partial(start_kernel, first, pair.shape[0]), gri...  21.7 us
    pallas_call x2, Pallas kernels, end_call(): pl.pallas_call(kernel, grid=(count,), in_specs=in_specs, out_specs=pl.Blo...  17.3 us
    pallas_call x3, Pallas kernels, product_call(): pl.pallas_call(functools.partial(product_kernel, update, len(lefts), len(...  15.7 us
  transfers between devices with their start and end apart: 5, of which 5 were waited for; matrix products, arithmetic and copies ran while one was open for 0% of the time, Pallas kernels for 10%

profile of v4, /device:TPU:9, one launch (start us, length us, event | category | flops | bytes accessed | tf_op | source)
XLA Modules:
  0.0 630.5 jit_solution(4304164853736513660)
XLA Ops:
  0.0 1.1 copy.10
  1.1 0.7 slice_bitcast_fusion
  1.8 6.6 %shard_map.73 = bf16[16,2,8,16,256]{4,3,2,1,0:T(8,128)(2,1)} custom-call(s32[512]{0:T(512)} %refs_0_.1, bf16[64,256,128]{2,1,0:T(8,128)(2,1)} %refs_2_.1, s32[64,256]{1,0:T(8,128)} %refs_3_.1, s32[1,512]{1,0:T(1,128)} %bitcast.48, f32[2,128]{1,0:T(2,128)} %refs_5_.1, bf16[512,128]{1,0:T(8,128)(2,1)} %get-tuple-element.18.proj_ref), custom_call_target="tpu_custom_call" | custom-call | flops 671088640 | bytes 2097152 | tf_op jit(solution)/shard_map/pallas_call | solution.py:185
  8.5 6.6 %all-to-all-start = ((bf16[16,2,8,16,256]{4,3,2,1,0:T(8,128)(2,1)}), bf16[16,2,8,16,256]{4,3,2,1,0:T(8,128)(2,1)S(1)}, u32[]{:S(2)}, u32[]{:S(2)}) async-start(bf16[16,2,8,16,256]{4,3,2,1,0:T(8,128)(2,1)} %shard_map.73), calls=%async_computation | async-start | bytes 4194304 | tf_op jit(solution)/shard_map/all_to_all | solution.py:359
  15.0 15.1 %shard_map.74 = bf16[16,2,8,48,256]{4,3,2,1,0:T(8,128)(2,1)} custom-call(s32[512]{0:T(512)} %refs_0_.1, bf16[64,256,128]{2,1,0:T(8,128)(2,1)} %refs_2_.1, s32[64,256]{1,0:T(8,128)} %refs_3_.1, s32[1,512]{1,0:T(1,128)} %bitcast.49, f32[2,128]{1,0:T(2,128)} %refs_5_.1, bf16[512,128]{1,0:T(8,128)(2,1)} %get-tuple-element.18.proj_ref), custom_call_target="tpu_custom_call" | custom-call | flops 2013265920 | bytes 6291456 | tf_op jit(solution)/shard_map/pallas_call | solution.py:185
  30.1 33.2 %all-to-all-done = bf16[16,2,8,16,256]{4,3,2,1,0:T(8,128)(2,1)S(1)} async-done(((bf16[16,2,8,16,256]{4,3,2,1,0:T(8,128)(2,1)}), bf16[16,2,8,16,256]{4,3,2,1,0:T(8,128)(2,1)S(1)}, u32[]{:S(2)}, u32[]{:S(2)}) %all-to-all-start) | async-done | bytes 2097184 | tf_op jit(solution)/shard_map/all_to_all | solution.py:359
  63.3 142.5 %all_to_all.40 = bf16[16,2,8,48,256]{4,3,2,1,0:T(8,128)(2,1)} all-to-all(bf16[16,2,8,48,256]{4,3,2,1,0:T(8,128)(2,1)} %shard_map.74), channel_id=1, replica_groups=mesh['grp'=2,'row'=8,'chan'=2] {'row','chan'}, dimensions={0} | all-to-all | bytes 12582912 | tf_op jit(solution)/shard_map/all_to_all | solution.py:359
  205.9 0.0 copy-done
  205.9 4.2 shard_map.75
  210.0 4.2 all-to-all-start.2
  214.2 5.3 shard_map.77
  219.5 20.4 %all-to-all-done.2 = bf16[16,8,16,256]{3,2,1,0:T(8,128)(2,1)S(1)} async-done(((bf16[16,8,16,256]{3,2,1,0:T(8,128)(2,1)}), bf16[16,8,16,256]{3,2,1,0:T(8,128)(2,1)S(1)}, u32[]{:S(2)}, u32[]{:S(2)}) %all-to-all-start.2) | async-done | bytes 1048608 | tf_op jit(solution)/shard_map/all_to_all | solution.py:359
  239.9 1.1 copy-done.4
  241.0 4.0 all-to-all-start.4
  245.0 0.1 copy.11
  245.1 0.0 copy-done.6
  245.1 0.1 copy.12
  245.2 0.7 slice_bitcast_fusion.2
  245.9 9.8 %shard_map.76 = (f32[64,128,256]{2,1,0:T(8,128)}, bf16[16,2,8,16,256]{4,3,2,1,0:T(8,128)(2,1)}) custom-call(s32[512]{0:T(512)} %refs_0_.1, bf16[128,16,256]{2,1,0:T(8,128)(2,1)} %bitcast.42, bf16[64,256,128]{2,1,0:T(8,128)(2,1)} %refs_2_.1, s32[64,256]{1,0:T(8,128)} %refs_3_.1, s32[1,512]{1,0:T(1,128)} %bitcast.50, f32[2,128]{1,0:T(2,128)} %refs_5_.1, ...), custom_call_target="tpu_custom_call" | custom-call | flops 1073741824 | bytes 6291456 | tf_op jit(solution)/shard_map/pallas_call | solution.py:227
  255.7 60.0 %all-to-all-done.4 = bf16[16,8,48,256]{3,2,1,0:T(8,128)(2,1)S(1)} async-done(((bf16[16,8,48,256]{3,2,1,0:T(8,128)(2,1)}), bf16[16,8,48,256]{3,2,1,0:T(8,128)(2,1)S(1)}, u32[]{:S(2)}, u32[]{:S(2)}) %all-to-all-start.4) | async-done | bytes 3145760 | tf_op jit(solution)/shard_map/all_to_all | solution.py:359
  315.7 1.7 copy-done.2
  317.4 4.4 all-to-all-start.3
  321.7 24.3 %shard_map.78 = (f32[64,128,256]{2,1,0:T(8,128)}, bf16[16,2,8,48,256]{4,3,2,1,0:T(8,128)(2,1)}) custom-call(s32[512]{0:T(512)} %refs_0_.1, bf16[128,48,256]{2,1,0:T(8,128)(2,1)} %bitcast.38, bf16[64,256,128]{2,1,0:T(8,128)(2,1)} %refs_2_.1, s32[64,256]{1,0:T(8,128)} %refs_3_.1, s32[1,512]{1,0:T(1,128)} %bitcast.51, ...), custom_call_target="tpu_custom_call", output_to_operand_aliasing={{0}: (9, {})} | custom-call | flops 3221225472 | bytes 18874368 | tf_op jit(solution)/shard_map/pallas_call | solution.py:227
  346.1 24.0 %all-to-all-done.3 = bf16[16,2,8,16,256]{4,3,2,1,0:T(8,128)(2,1)S(1)} async-done(((bf16[16,2,8,16,256]{4,3,2,1,0:T(8,128)(2,1)}), bf16[16,2,8,16,256]{4,3,2,1,0:T(8,128)(2,1)S(1)}, u32[]{:S(2)}, u32[]{:S(2)}) %all-to-all-start.3) | async-done | bytes 2097184 | tf_op jit(solution)/shard_map/all_to_all | solution.py:359
  370.0 142.5 %all_to_all.41 = bf16[16,2,8,48,256]{4,3,2,1,0:T(8,128)(2,1)} all-to-all(bf16[16,2,8,48,256]{4,3,2,1,0:T(8,128)(2,1)} %get-tuple-element.13), channel_id=1, replica_groups=mesh['grp'=2,'row'=8,'chan'=2] {'row','chan'}, dimensions={0} | all-to-all | bytes 12582912 | tf_op jit(solution)/shard_map/all_to_all | solution.py:359
  512.6 6.2 shard_map.79
  518.7 75.2 %all_to_all.42 = bf16[16,8,48,256]{3,2,1,0:T(8,128)(2,1)} all-to-all(bf16[16,8,48,256]{3,2,1,0:T(8,128)(2,1)} %bitcast.44), channel_id=1, replica_groups=mesh['grp'=2,'row'=8,'chan'=2] {'row','chan'}, dimensions={0} | all-to-all | bytes 6291456 | tf_op jit(solution)/shard_map/all_to_all | solution.py:359
  593.9 4.1 all-to-all-start.6
  598.0 11.6 %shard_map.80.earlier_ref = bf16[64,256,128]{2,1,0:T(8,128)(2,1)} custom-call(bf16[128,48,256]{2,1,0:T(8,128)(2,1)} %bitcast.40, f32[64,128,256]{2,1,0:T(8,128)} %get-tuple-element.15.state_ref, bf16[128,128]{1,0:T(8,128)(2,1)} %get-tuple-element.24.gate_ref, bf16[128,128]{1,0:T(8,128)(2,1)} %get-tuple-element.19.back_ref), custom_call_target="tpu_custom_call" | custom-call | flops 805306368 | bytes 12582912 | tf_op jit(solution)/shard_map/pallas_call | solution.py:263
  609.6 14.1 %all-to-all-done.6 = bf16[16,8,16,256]{3,2,1,0:T(8,128)(2,1)S(1)} async-done(((bf16[16,8,16,256]{3,2,1,0:T(8,128)(2,1)}), bf16[16,8,16,256]{3,2,1,0:T(8,128)(2,1)S(1)}, u32[]{:S(2)}, u32[]{:S(2)}) %all-to-all-start.6) | async-done | bytes 1048608 | tf_op jit(solution)/shard_map/all_to_all | solution.py:359
  623.8 1.1 copy-done.3
  624.9 5.7 shard_map.81
  (9 shorter events, 0.0 us)
Async XLA Ops:
  8.5 54.9 %all-to-all-start = ((bf16[16,2,8,16,256]{4,3,2,1,0:T(8,128)(2,1)}), bf16[16,2,8,16,256]{4,3,2,1,0:T(8,128)(2,1)S(1)}, u32[]{:S(2)}, u32[]{:S(2)}) async-start(bf16[16,2,8,16,256]{4,3,2,1,0:T(8,128)(2,1)} %shard_map.73), calls=%async_computation | async-start | bytes 4194304 | tf_op jit(solution)/shard_map/all_to_all | solution.py:359
  63.3 142.5 %copy-start = (bf16[16,2,8,16,256]{4,3,2,1,0:T(8,128)(2,1)}, bf16[16,2,8,16,256]{4,3,2,1,0:T(8,128)(2,1)S(1)}, u32[]{:S(2)}) copy-start(bf16[16,2,8,16,256]{4,3,2,1,0:T(8,128)(2,1)S(1)} %all-to-all-done) | copy-start | bytes 6291460
  210.0 29.9 %all-to-all-start.2 = ((bf16[16,8,16,256]{3,2,1,0:T(8,128)(2,1)}), bf16[16,8,16,256]{3,2,1,0:T(8,128)(2,1)S(1)}, u32[]{:S(2)}, u32[]{:S(2)}) async-start(bf16[16,8,16,256]{3,2,1,0:T(8,128)(2,1)} %bitcast.43), calls=%async_computation.2 | async-start | bytes 2097152 | tf_op jit(solution)/shard_map/all_to_all | solution.py:359
  219.5 25.5 %copy-start.5 = (bf16[2,128,128]{2,1,0:T(8,128)(2,1)S(1)}, bf16[2,128,128]{2,1,0:T(8,128)(2,1)}, u32[]{:S(2)}) copy-start(bf16[2,128,128]{2,1,0:T(8,128)(2,1)} %param.12) | copy-start | bytes 196612
  219.5 25.6 %copy-start.6 = (bf16[2,128,128]{2,1,0:T(8,128)(2,1)S(1)}, bf16[2,128,128]{2,1,0:T(8,128)(2,1)}, u32[]{:S(2)}) copy-start(bf16[2,128,128]{2,1,0:T(8,128)(2,1)} %param.13) | copy-start | bytes 196612
  239.9 1.1 copy-start.4
  241.0 74.7 %all-to-all-start.4 = ((bf16[16,8,48,256]{3,2,1,0:T(8,128)(2,1)}), bf16[16,8,48,256]{3,2,1,0:T(8,128)(2,1)S(1)}, u32[]{:S(2)}, u32[]{:S(2)}) async-start(bf16[16,8,48,256]{3,2,1,0:T(8,128)(2,1)} %bitcast.39), calls=%async_computation.4 | async-start | bytes 6291456 | tf_op jit(solution)/shard_map/all_to_all | solution.py:359
  315.7 1.7 copy-start.2
  317.4 52.6 %all-to-all-start.3 = ((bf16[16,2,8,16,256]{4,3,2,1,0:T(8,128)(2,1)}), bf16[16,2,8,16,256]{4,3,2,1,0:T(8,128)(2,1)S(1)}, u32[]{:S(2)}, u32[]{:S(2)}) async-start(bf16[16,2,8,16,256]{4,3,2,1,0:T(8,128)(2,1)} %get-tuple-element.11), calls=%async_computation.3 | async-start | bytes 4194304 | tf_op jit(solution)/shard_map/all_to_all | solution.py:359
  370.0 142.5 %copy-start.1 = (bf16[16,2,8,16,256]{4,3,2,1,0:T(8,128)(2,1)}, bf16[16,2,8,16,256]{4,3,2,1,0:T(8,128)(2,1)S(1)}, u32[]{:S(2)}) copy-start(bf16[16,2,8,16,256]{4,3,2,1,0:T(8,128)(2,1)S(1)} %all-to-all-done.3) | copy-start | bytes 6291460
  593.9 29.9 %all-to-all-start.6 = ((bf16[16,8,16,256]{3,2,1,0:T(8,128)(2,1)}), bf16[16,8,16,256]{3,2,1,0:T(8,128)(2,1)S(1)}, u32[]{:S(2)}, u32[]{:S(2)}) async-start(bf16[16,8,16,256]{3,2,1,0:T(8,128)(2,1)} %bitcast.16), calls=%async_computation.6 | async-start | bytes 2097152 | tf_op jit(solution)/shard_map/all_to_all | solution.py:359
  623.8 1.1 copy-start.3

commit v5 on v4

--- a/solution.py
+++ b/solution.py
@@ -76,16 +76,19 @@
     for side, scratch in enumerate((left_scr, right_scr)):
         for part in range(cols // LANES):
             out_ref[:, side, :, :, part * LANES : (part + 1) * LANES] = (
-                scratch[part].astype(jnp.bfloat16).reshape(targets, share, rows, LANES)
+                scratch[part, : targets * share * rows, :]
+                .astype(jnp.bfloat16)
+                .reshape(targets, share, rows, LANES)
             )
 
 
 def read_mixed(mixed_ref, scratch):
+    used = mixed_ref.shape[0] * mixed_ref.shape[1]
     for part in range(scratch.shape[0]):
-        scratch[part] = (
+        scratch[part, :used, :] = (
             mixed_ref[:, :, part * LANES : (part + 1) * LANES]
             .astype(jnp.float32)
-            .reshape(scratch.shape[1:])
+            .reshape(used, LANES)
         )
 
 
@@ -172,7 +175,7 @@
 
 
 def scratches(count, channels, rows, cols):
-    return [pltpu.VMEM((cols // LANES, channels * rows, LANES), jnp.float32)] * count
+    return [pltpu.VMEM((cols // LANES, (channels + 1) * rows, LANES), jnp.float32)] * count
 
 
 SMEM_SPEC = pl.BlockSpec(memory_space=pltpu.SMEM)

time: 631 us -> 631 us (level)
  no operation moved by 1% of the time
where the time goes in v5:
time: 631 us
  blocking collectives  360 us (57%)
  waiting for transfers between devices  152 us (24%)
  Pallas kernels  88.8 us (14%)
  starting transfers between devices  23.2 us (4%)
  local copies, waits for them, and re-layouts  6.56 us (1%)
    all_to_all x3, blocking collectives, exchange(): lax.all_to_all(array, ('row', 'chan'), split_axis=0, concat_axis=0, tiled...  360 us
    all_to_all x5, waiting for transfers between devices, exchange(): lax.all_to_all(array, ('row', 'chan'), split_axis=0, concat_axis=0, tiled...  152 us
    pallas_call x2, Pallas kernels, middle_call(): pl.pallas_call(functools.partial(kernel, first, rows), grid=(count,), in_...  34.1 us
    all_to_all x5, starting transfers between devices, exchange(): lax.all_to_all(array, ('row', 'chan'), split_axis=0, concat_axis=0, tiled...  23.2 us
    pallas_call x2, Pallas kernels, start_call(): pl.pallas_call(functools.partial(start_kernel, first, pair.shape[0]), gri...  21.7 us
    pallas_call x2, Pallas kernels, end_call(): pl.pallas_call(kernel, grid=(count,), in_specs=in_specs, out_specs=pl.Blo...  17.3 us
    pallas_call x3, Pallas kernels, product_call(): pl.pallas_call(functools.partial(product_kernel, update, len(lefts), len(...  15.7 us
  transfers between devices with their start and end apart: 5, of which 5 were waited for; matrix products, arithmetic and copies ran while one was open for 0% of the time, Pallas kernels for 10%

profile of v5, /device:TPU:9, one launch (start us, length us, event | category | flops | bytes accessed | tf_op | source)
XLA Modules:
  0.0 630.6 jit_solution(65808493113074510)
XLA Ops:
  0.0 1.1 copy.10
  1.1 0.7 slice_bitcast_fusion
  1.8 6.6 %shard_map.73 = bf16[16,2,8,16,256]{4,3,2,1,0:T(8,128)(2,1)} custom-call(s32[512]{0:T(512)} %refs_0_.1, bf16[64,256,128]{2,1,0:T(8,128)(2,1)} %refs_2_.1, s32[64,256]{1,0:T(8,128)} %refs_3_.1, s32[1,512]{1,0:T(1,128)} %bitcast.48, f32[2,128]{1,0:T(2,128)} %refs_5_.1, bf16[512,128]{1,0:T(8,128)(2,1)} %get-tuple-element.18.proj_ref), custom_call_target="tpu_custom_call" | custom-call | flops 671088640 | bytes 2097152 | tf_op jit(solution)/shard_map/pallas_call | solution.py:188
  8.5 6.6 %all-to-all-start = ((bf16[16,2,8,16,256]{4,3,2,1,0:T(8,128)(2,1)}), bf16[16,2,8,16,256]{4,3,2,1,0:T(8,128)(2,1)S(1)}, u32[]{:S(2)}, u32[]{:S(2)}) async-start(bf16[16,2,8,16,256]{4,3,2,1,0:T(8,128)(2,1)} %shard_map.73), calls=%async_computation | async-start | bytes 4194304 | tf_op jit(solution)/shard_map/all_to_all | solution.py:362
  15.0 15.1 %shard_map.74 = bf16[16,2,8,48,256]{4,3,2,1,0:T(8,128)(2,1)} custom-call(s32[512]{0:T(512)} %refs_0_.1, bf16[64,256,128]{2,1,0:T(8,128)(2,1)} %refs_2_.1, s32[64,256]{1,0:T(8,128)} %refs_3_.1, s32[1,512]{1,0:T(1,128)} %bitcast.49, f32[2,128]{1,0:T(2,128)} %refs_5_.1, bf16[512,128]{1,0:T(8,128)(2,1)} %get-tuple-element.18.proj_ref), custom_call_target="tpu_custom_call" | custom-call | flops 2013265920 | bytes 6291456 | tf_op jit(solution)/shard_map/pallas_call | solution.py:188
  30.1 33.2 %all-to-all-done = bf16[16,2,8,16,256]{4,3,2,1,0:T(8,128)(2,1)S(1)} async-done(((bf16[16,2,8,16,256]{4,3,2,1,0:T(8,128)(2,1)}), bf16[16,2,8,16,256]{4,3,2,1,0:T(8,128)(2,1)S(1)}, u32[]{:S(2)}, u32[]{:S(2)}) %all-to-all-start) | async-done | bytes 2097184 | tf_op jit(solution)/shard_map/all_to_all | solution.py:362
  63.3 142.5 %all_to_all.40 = bf16[16,2,8,48,256]{4,3,2,1,0:T(8,128)(2,1)} all-to-all(bf16[16,2,8,48,256]{4,3,2,1,0:T(8,128)(2,1)} %shard_map.74), channel_id=1, replica_groups=mesh['grp'=2,'row'=8,'chan'=2] {'row','chan'}, dimensions={0} | all-to-all | bytes 12582912 | tf_op jit(solution)/shard_map/all_to_all | solution.py:362
  205.9 0.0 copy-done
  205.9 4.2 shard_map.75
  210.0 4.2 all-to-all-start.2
  214.2 5.3 shard_map.77
  219.5 20.4 %all-to-all-done.2 = bf16[16,8,16,256]{3,2,1,0:T(8,128)(2,1)S(1)} async-done(((bf16[16,8,16,256]{3,2,1,0:T(8,128)(2,1)}), bf16[16,8,16,256]{3,2,1,0:T(8,128)(2,1)S(1)}, u32[]{:S(2)}, u32[]{:S(2)}) %all-to-all-start.2) | async-done | bytes 1048608 | tf_op jit(solution)/shard_map/all_to_all | solution.py:362
  240.0 1.1 copy-done.4
  241.0 4.0 all-to-all-start.4
  245.0 0.1 copy.11
  245.1 0.0 copy-done.6
  245.1 0.1 copy.12
  245.2 0.7 slice_bitcast_fusion.2
  245.9 9.8 %shard_map.76 = (f32[64,128,256]{2,1,0:T(8,128)}, bf16[16,2,8,16,256]{4,3,2,1,0:T(8,128)(2,1)}) custom-call(s32[512]{0:T(512)} %refs_0_.1, bf16[128,16,256]{2,1,0:T(8,128)(2,1)} %bitcast.42, bf16[64,256,128]{2,1,0:T(8,128)(2,1)} %refs_2_.1, s32[64,256]{1,0:T(8,128)} %refs_3_.1, s32[1,512]{1,0:T(1,128)} %bitcast.50, f32[2,128]{1,0:T(2,128)} %refs_5_.1, ...), custom_call_target="tpu_custom_call" | custom-call | flops 1073741824 | bytes 6291456 | tf_op jit(solution)/shard_map/pallas_call | solution.py:230
  255.7 60.0 %all-to-all-done.4 = bf16[16,8,48,256]{3,2,1,0:T(8,128)(2,1)S(1)} async-done(((bf16[16,8,48,256]{3,2,1,0:T(8,128)(2,1)}), bf16[16,8,48,256]{3,2,1,0:T(8,128)(2,1)S(1)}, u32[]{:S(2)}, u32[]{:S(2)}) %all-to-all-start.4) | async-done | bytes 3145760 | tf_op jit(solution)/shard_map/all_to_all | solution.py:362
  315.7 1.7 copy-done.2
  317.4 4.4 all-to-all-start.3
  321.8 24.3 %shard_map.78 = (f32[64,128,256]{2,1,0:T(8,128)}, bf16[16,2,8,48,256]{4,3,2,1,0:T(8,128)(2,1)}) custom-call(s32[512]{0:T(512)} %refs_0_.1, bf16[128,48,256]{2,1,0:T(8,128)(2,1)} %bitcast.38, bf16[64,256,128]{2,1,0:T(8,128)(2,1)} %refs_2_.1, s32[64,256]{1,0:T(8,128)} %refs_3_.1, s32[1,512]{1,0:T(1,128)} %bitcast.51, ...), custom_call_target="tpu_custom_call", output_to_operand_aliasing={{0}: (9, {})} | custom-call | flops 3221225472 | bytes 18874368 | tf_op jit(solution)/shard_map/pallas_call | solution.py:230
  346.1 24.0 %all-to-all-done.3 = bf16[16,2,8,16,256]{4,3,2,1,0:T(8,128)(2,1)S(1)} async-done(((bf16[16,2,8,16,256]{4,3,2,1,0:T(8,128)(2,1)}), bf16[16,2,8,16,256]{4,3,2,1,0:T(8,128)(2,1)S(1)}, u32[]{:S(2)}, u32[]{:S(2)}) %all-to-all-start.3) | async-done | bytes 2097184 | tf_op jit(solution)/shard_map/all_to_all | solution.py:362
  370.0 142.5 %all_to_all.41 = bf16[16,2,8,48,256]{4,3,2,1,0:T(8,128)(2,1)} all-to-all(bf16[16,2,8,48,256]{4,3,2,1,0:T(8,128)(2,1)} %get-tuple-element.13), channel_id=1, replica_groups=mesh['grp'=2,'row'=8,'chan'=2] {'row','chan'}, dimensions={0} | all-to-all | bytes 12582912 | tf_op jit(solution)/shard_map/all_to_all | solution.py:362
  512.6 6.2 shard_map.79
  518.7 75.2 %all_to_all.42 = bf16[16,8,48,256]{3,2,1,0:T(8,128)(2,1)} all-to-all(bf16[16,8,48,256]{3,2,1,0:T(8,128)(2,1)} %bitcast.44), channel_id=1, replica_groups=mesh['grp'=2,'row'=8,'chan'=2] {'row','chan'}, dimensions={0} | all-to-all | bytes 6291456 | tf_op jit(solution)/shard_map/all_to_all | solution.py:362
  593.9 4.1 all-to-all-start.6
  598.0 11.6 %shard_map.80.earlier_ref = bf16[64,256,128]{2,1,0:T(8,128)(2,1)} custom-call(bf16[128,48,256]{2,1,0:T(8,128)(2,1)} %bitcast.40, f32[64,128,256]{2,1,0:T(8,128)} %get-tuple-element.15.state_ref, bf16[128,128]{1,0:T(8,128)(2,1)} %get-tuple-element.24.gate_ref, bf16[128,128]{1,0:T(8,128)(2,1)} %get-tuple-element.19.back_ref), custom_call_target="tpu_custom_call" | custom-call | flops 805306368 | bytes 12582912 | tf_op jit(solution)/shard_map/pallas_call | solution.py:266
  609.7 14.1 %all-to-all-done.6 = bf16[16,8,16,256]{3,2,1,0:T(8,128)(2,1)S(1)} async-done(((bf16[16,8,16,256]{3,2,1,0:T(8,128)(2,1)}), bf16[16,8,16,256]{3,2,1,0:T(8,128)(2,1)S(1)}, u32[]{:S(2)}, u32[]{:S(2)}) %all-to-all-start.6) | async-done | bytes 1048608 | tf_op jit(solution)/shard_map/all_to_all | solution.py:362
  623.8 1.1 copy-done.3
  624.9 5.7 shard_map.81
  (9 shorter events, 0.0 us)
Async XLA Ops:
  8.5 54.9 %all-to-all-start = ((bf16[16,2,8,16,256]{4,3,2,1,0:T(8,128)(2,1)}), bf16[16,2,8,16,256]{4,3,2,1,0:T(8,128)(2,1)S(1)}, u32[]{:S(2)}, u32[]{:S(2)}) async-start(bf16[16,2,8,16,256]{4,3,2,1,0:T(8,128)(2,1)} %shard_map.73), calls=%async_computation | async-start | bytes 4194304 | tf_op jit(solution)/shard_map/all_to_all | solution.py:362
  63.3 142.5 %copy-start = (bf16[16,2,8,16,256]{4,3,2,1,0:T(8,128)(2,1)}, bf16[16,2,8,16,256]{4,3,2,1,0:T(8,128)(2,1)S(1)}, u32[]{:S(2)}) copy-start(bf16[16,2,8,16,256]{4,3,2,1,0:T(8,128)(2,1)S(1)} %all-to-all-done) | copy-start | bytes 6291460
  210.0 29.9 %all-to-all-start.2 = ((bf16[16,8,16,256]{3,2,1,0:T(8,128)(2,1)}), bf16[16,8,16,256]{3,2,1,0:T(8,128)(2,1)S(1)}, u32[]{:S(2)}, u32[]{:S(2)}) async-start(bf16[16,8,16,256]{3,2,1,0:T(8,128)(2,1)} %bitcast.43), calls=%async_computation.2 | async-start | bytes 2097152 | tf_op jit(solution)/shard_map/all_to_all | solution.py:362
  219.5 25.5 %copy-start.5 = (bf16[2,128,128]{2,1,0:T(8,128)(2,1)S(1)}, bf16[2,128,128]{2,1,0:T(8,128)(2,1)}, u32[]{:S(2)}) copy-start(bf16[2,128,128]{2,1,0:T(8,128)(2,1)} %param.12) | copy-start | bytes 196612
  219.5 25.6 %copy-start.6 = (bf16[2,128,128]{2,1,0:T(8,128)(2,1)S(1)}, bf16[2,128,128]{2,1,0:T(8,128)(2,1)}, u32[]{:S(2)}) copy-start(bf16[2,128,128]{2,1,0:T(8,128)(2,1)} %param.13) | copy-start | bytes 196612
  240.0 1.1 copy-start.4
  241.0 74.7 %all-to-all-start.4 = ((bf16[16,8,48,256]{3,2,1,0:T(8,128)(2,1)}), bf16[16,8,48,256]{3,2,1,0:T(8,128)(2,1)S(1)}, u32[]{:S(2)}, u32[]{:S(2)}) async-start(bf16[16,8,48,256]{3,2,1,0:T(8,128)(2,1)} %bitcast.39), calls=%async_computation.4 | async-start | bytes 6291456 | tf_op jit(solution)/shard_map/all_to_all | solution.py:362
  315.7 1.7 copy-start.2
  317.4 52.6 %all-to-all-start.3 = ((bf16[16,2,8,16,256]{4,3,2,1,0:T(8,128)(2,1)}), bf16[16,2,8,16,256]{4,3,2,1,0:T(8,128)(2,1)S(1)}, u32[]{:S(2)}, u32[]{:S(2)}) async-start(bf16[16,2,8,16,256]{4,3,2,1,0:T(8,128)(2,1)} %get-tuple-element.11), calls=%async_computation.3 | async-start | bytes 4194304 | tf_op jit(solution)/shard_map/all_to_all | solution.py:362
  370.0 142.5 %copy-start.1 = (bf16[16,2,8,16,256]{4,3,2,1,0:T(8,128)(2,1)}, bf16[16,2,8,16,256]{4,3,2,1,0:T(8,128)(2,1)S(1)}, u32[]{:S(2)}) copy-start(bf16[16,2,8,16,256]{4,3,2,1,0:T(8,128)(2,1)S(1)} %all-to-all-done.3) | copy-start | bytes 6291460
  593.9 29.9 %all-to-all-start.6 = ((bf16[16,8,16,256]{3,2,1,0:T(8,128)(2,1)}), bf16[16,8,16,256]{3,2,1,0:T(8,128)(2,1)S(1)}, u32[]{:S(2)}, u32[]{:S(2)}) async-start(bf16[16,8,16,256]{3,2,1,0:T(8,128)(2,1)} %bitcast.16), calls=%async_computation.6 | async-start | bytes 2097152 | tf_op jit(solution)/shard_map/all_to_all | solution.py:362
  623.8 1.1 copy-start.3

commit v6 on v5

--- a/solution.py
+++ b/solution.py
@@ -99,7 +99,7 @@
     step = pl.program_id(0) + first
     turn_embed(embed_ref, embed_scr)
 
-    @pl.loop(0, rows, unroll=4)
+    @pl.loop(0, rows, unroll=8)
     def _(i):
         same = same_chain(row_chain, col_chain, pair_ref.shape[1], total_rows, step * rows + i)
         state = first_state(pair_ref, same, embed_scr, i)
@@ -120,7 +120,7 @@
     turn_embed(embed_ref, embed_scr)
     read_mixed(mixed_ref, mixed_scr)
 
-    @pl.loop(0, rows, unroll=4)
+    @pl.loop(0, rows, unroll=8)
     def _(i):
         same = same_chain(row_chain, col_chain, pair_ref.shape[1], total_rows, step * rows + i)
         state = first_state(pair_ref, same, embed_scr, i)
@@ -141,7 +141,7 @@
     channels = mixed_ref.shape[0]
     read_mixed(mixed_ref, mixed_scr)
 
-    @pl.loop(0, rows, unroll=4)
+    @pl.loop(0, rows, unroll=8)
     def _(i):
         state = state_ref[i]
         normed = norm_channels(state).astype(jnp.bfloat16)

time: 631 us -> 630 us (level)
  no operation moved by 1% of the time
where the time goes in v6:
time: 630 us
  blocking collectives  360 us (57%)
  waiting for transfers between devices  157 us (25%)
  Pallas kernels  82.5 us (13%)
  starting transfers between devices  23.2 us (4%)
  local copies, waits for them, and re-layouts  6.56 us (1%)
    all_to_all x3, blocking collectives, exchange(): lax.all_to_all(array, ('row', 'chan'), split_axis=0, concat_axis=0, tiled...  360 us
    all_to_all x5, waiting for transfers between devices, exchange(): lax.all_to_all(array, ('row', 'chan'), split_axis=0, concat_axis=0, tiled...  157 us
    pallas_call x2, Pallas kernels, middle_call(): pl.pallas_call(functools.partial(kernel, first, rows), grid=(count,), in_...  31.1 us
    all_to_all x5, starting transfers between devices, exchange(): lax.all_to_all(array, ('row', 'chan'), split_axis=0, concat_axis=0, tiled...  23.2 us
    pallas_call x2, Pallas kernels, start_call(): pl.pallas_call(functools.partial(start_kernel, first, pair.shape[0]), gri...  19.1 us
    pallas_call x2, Pallas kernels, end_call(): pl.pallas_call(kernel, grid=(count,), in_specs=in_specs, out_specs=pl.Blo...  16.7 us
    pallas_call x3, Pallas kernels, product_call(): pl.pallas_call(functools.partial(product_kernel, update, len(lefts), len(...  15.6 us
  transfers between devices with their start and end apart: 5, of which 5 were waited for; matrix products, arithmetic and copies ran while one was open for 0% of the time, Pallas kernels for 10%

profile of v6, /device:TPU:9, one launch (start us, length us, event | category | flops | bytes accessed | tf_op | source)
XLA Modules:
  0.0 629.7 jit_solution(1258465472059068686)
XLA Ops:
  0.0 1.1 copy.10
  1.1 0.7 slice_bitcast_fusion
  1.8 6.0 shard_map.73
  7.8 6.6 %all-to-all-start = ((bf16[16,2,8,16,256]{4,3,2,1,0:T(8,128)(2,1)}), bf16[16,2,8,16,256]{4,3,2,1,0:T(8,128)(2,1)S(1)}, u32[]{:S(2)}, u32[]{:S(2)}) async-start(bf16[16,2,8,16,256]{4,3,2,1,0:T(8,128)(2,1)} %shard_map.73), calls=%async_computation | async-start | bytes 4194304 | tf_op jit(solution)/shard_map/all_to_all | solution.py:362
  14.4 13.1 %shard_map.74 = bf16[16,2,8,48,256]{4,3,2,1,0:T(8,128)(2,1)} custom-call(s32[512]{0:T(512)} %refs_0_.1, bf16[64,256,128]{2,1,0:T(8,128)(2,1)} %refs_2_.1, s32[64,256]{1,0:T(8,128)} %refs_3_.1, s32[1,512]{1,0:T(1,128)} %bitcast.49, f32[2,128]{1,0:T(2,128)} %refs_5_.1, bf16[512,128]{1,0:T(8,128)(2,1)} %get-tuple-element.18.proj_ref), custom_call_target="tpu_custom_call" | custom-call | flops 2013265920 | bytes 6291456 | tf_op jit(solution)/shard_map/pallas_call | solution.py:188
  27.5 35.2 %all-to-all-done = bf16[16,2,8,16,256]{4,3,2,1,0:T(8,128)(2,1)S(1)} async-done(((bf16[16,2,8,16,256]{4,3,2,1,0:T(8,128)(2,1)}), bf16[16,2,8,16,256]{4,3,2,1,0:T(8,128)(2,1)S(1)}, u32[]{:S(2)}, u32[]{:S(2)}) %all-to-all-start) | async-done | bytes 2097184 | tf_op jit(solution)/shard_map/all_to_all | solution.py:362
  62.7 142.5 %all_to_all.40 = bf16[16,2,8,48,256]{4,3,2,1,0:T(8,128)(2,1)} all-to-all(bf16[16,2,8,48,256]{4,3,2,1,0:T(8,128)(2,1)} %shard_map.74), channel_id=1, replica_groups=mesh['grp'=2,'row'=8,'chan'=2] {'row','chan'}, dimensions={0} | all-to-all | bytes 12582912 | tf_op jit(solution)/shard_map/all_to_all | solution.py:362
  205.2 0.0 copy-done
  205.2 4.2 shard_map.75
  209.4 4.2 all-to-all-start.2
  213.6 5.3 shard_map.77
  218.9 20.4 %all-to-all-done.2 = bf16[16,8,16,256]{3,2,1,0:T(8,128)(2,1)S(1)} async-done(((bf16[16,8,16,256]{3,2,1,0:T(8,128)(2,1)}), bf16[16,8,16,256]{3,2,1,0:T(8,128)(2,1)S(1)}, u32[]{:S(2)}, u32[]{:S(2)}) %all-to-all-start.2) | async-done | bytes 1048608 | tf_op jit(solution)/shard_map/all_to_all | solution.py:362
  239.3 1.1 copy-done.4
  240.4 4.0 all-to-all-start.4
  244.3 0.1 copy.11
  244.5 0.0 copy-done.6
  244.5 0.1 copy.12
  244.6 0.7 slice_bitcast_fusion.2
  245.3 9.2 %shard_map.76 = (f32[64,128,256]{2,1,0:T(8,128)}, bf16[16,2,8,16,256]{4,3,2,1,0:T(8,128)(2,1)}) custom-call(s32[512]{0:T(512)} %refs_0_.1, bf16[128,16,256]{2,1,0:T(8,128)(2,1)} %bitcast.42, bf16[64,256,128]{2,1,0:T(8,128)(2,1)} %refs_2_.1, s32[64,256]{1,0:T(8,128)} %refs_3_.1, s32[1,512]{1,0:T(1,128)} %bitcast.50, f32[2,128]{1,0:T(2,128)} %refs_5_.1, ...), custom_call_target="tpu_custom_call" | custom-call | flops 1073741824 | bytes 6291456 | tf_op jit(solution)/shard_map/pallas_call | solution.py:230
  254.5 60.6 %all-to-all-done.4 = bf16[16,8,48,256]{3,2,1,0:T(8,128)(2,1)S(1)} async-done(((bf16[16,8,48,256]{3,2,1,0:T(8,128)(2,1)}), bf16[16,8,48,256]{3,2,1,0:T(8,128)(2,1)S(1)}, u32[]{:S(2)}, u32[]{:S(2)}) %all-to-all-start.4) | async-done | bytes 3145760 | tf_op jit(solution)/shard_map/all_to_all | solution.py:362
  315.1 1.7 copy-done.2
  316.7 4.4 all-to-all-start.3
  321.1 21.9 %shard_map.78 = (f32[64,128,256]{2,1,0:T(8,128)}, bf16[16,2,8,48,256]{4,3,2,1,0:T(8,128)(2,1)}) custom-call(s32[512]{0:T(512)} %refs_0_.1, bf16[128,48,256]{2,1,0:T(8,128)(2,1)} %bitcast.38, bf16[64,256,128]{2,1,0:T(8,128)(2,1)} %refs_2_.1, s32[64,256]{1,0:T(8,128)} %refs_3_.1, s32[1,512]{1,0:T(1,128)} %bitcast.51, ...), custom_call_target="tpu_custom_call", output_to_operand_aliasing={{0}: (9, {})} | custom-call | flops 3221225472 | bytes 18874368 | tf_op jit(solution)/shard_map/pallas_call | solution.py:230
  343.0 26.4 %all-to-all-done.3 = bf16[16,2,8,16,256]{4,3,2,1,0:T(8,128)(2,1)S(1)} async-done(((bf16[16,2,8,16,256]{4,3,2,1,0:T(8,128)(2,1)}), bf16[16,2,8,16,256]{4,3,2,1,0:T(8,128)(2,1)S(1)}, u32[]{:S(2)}, u32[]{:S(2)}) %all-to-all-start.3) | async-done | bytes 2097184 | tf_op jit(solution)/shard_map/all_to_all | solution.py:362
  369.4 142.5 %all_to_all.41 = bf16[16,2,8,48,256]{4,3,2,1,0:T(8,128)(2,1)} all-to-all(bf16[16,2,8,48,256]{4,3,2,1,0:T(8,128)(2,1)} %get-tuple-element.13), channel_id=1, replica_groups=mesh['grp'=2,'row'=8,'chan'=2] {'row','chan'}, dimensions={0} | all-to-all | bytes 12582912 | tf_op jit(solution)/shard_map/all_to_all | solution.py:362
  511.9 6.2 shard_map.79
  518.1 75.2 %all_to_all.42 = bf16[16,8,48,256]{3,2,1,0:T(8,128)(2,1)} all-to-all(bf16[16,8,48,256]{3,2,1,0:T(8,128)(2,1)} %bitcast.44), channel_id=1, replica_groups=mesh['grp'=2,'row'=8,'chan'=2] {'row','chan'}, dimensions={0} | all-to-all | bytes 6291456 | tf_op jit(solution)/shard_map/all_to_all | solution.py:362
  593.2 4.1 all-to-all-start.6
  597.4 11.1 %shard_map.80.earlier_ref = bf16[64,256,128]{2,1,0:T(8,128)(2,1)} custom-call(bf16[128,48,256]{2,1,0:T(8,128)(2,1)} %bitcast.40, f32[64,128,256]{2,1,0:T(8,128)} %get-tuple-element.15.state_ref, bf16[128,128]{1,0:T(8,128)(2,1)} %get-tuple-element.24.gate_ref, bf16[128,128]{1,0:T(8,128)(2,1)} %get-tuple-element.19.back_ref), custom_call_target="tpu_custom_call" | custom-call | flops 805306368 | bytes 12582912 | tf_op jit(solution)/shard_map/pallas_call | solution.py:266
  608.5 14.6 %all-to-all-done.6 = bf16[16,8,16,256]{3,2,1,0:T(8,128)(2,1)S(1)} async-done(((bf16[16,8,16,256]{3,2,1,0:T(8,128)(2,1)}), bf16[16,8,16,256]{3,2,1,0:T(8,128)(2,1)S(1)}, u32[]{:S(2)}, u32[]{:S(2)}) %all-to-all-start.6) | async-done | bytes 1048608 | tf_op jit(solution)/shard_map/all_to_all | solution.py:362
  623.1 1.1 copy-done.3
  624.2 5.5 shard_map.81
  (9 shorter events, 0.0 us)
Async XLA Ops:
  7.8 54.9 %all-to-all-start = ((bf16[16,2,8,16,256]{4,3,2,1,0:T(8,128)(2,1)}), bf16[16,2,8,16,256]{4,3,2,1,0:T(8,128)(2,1)S(1)}, u32[]{:S(2)}, u32[]{:S(2)}) async-start(bf16[16,2,8,16,256]{4,3,2,1,0:T(8,128)(2,1)} %shard_map.73), calls=%async_computation | async-start | bytes 4194304 | tf_op jit(solution)/shard_map/all_to_all | solution.py:362
  62.7 142.5 %copy-start = (bf16[16,2,8,16,256]{4,3,2,1,0:T(8,128)(2,1)}, bf16[16,2,8,16,256]{4,3,2,1,0:T(8,128)(2,1)S(1)}, u32[]{:S(2)}) copy-start(bf16[16,2,8,16,256]{4,3,2,1,0:T(8,128)(2,1)S(1)} %all-to-all-done) | copy-start | bytes 6291460
  209.4 29.9 %all-to-all-start.2 = ((bf16[16,8,16,256]{3,2,1,0:T(8,128)(2,1)}), bf16[16,8,16,256]{3,2,1,0:T(8,128)(2,1)S(1)}, u32[]{:S(2)}, u32[]{:S(2)}) async-start(bf16[16,8,16,256]{3,2,1,0:T(8,128)(2,1)} %bitcast.43), calls=%async_computation.2 | async-start | bytes 2097152 | tf_op jit(solution)/shard_map/all_to_all | solution.py:362
  218.9 25.5 %copy-start.5 = (bf16[2,128,128]{2,1,0:T(8,128)(2,1)S(1)}, bf16[2,128,128]{2,1,0:T(8,128)(2,1)}, u32[]{:S(2)}) copy-start(bf16[2,128,128]{2,1,0:T(8,128)(2,1)} %param.12) | copy-start | bytes 196612
  218.9 25.6 %copy-start.6 = (bf16[2,128,128]{2,1,0:T(8,128)(2,1)S(1)}, bf16[2,128,128]{2,1,0:T(8,128)(2,1)}, u32[]{:S(2)}) copy-start(bf16[2,128,128]{2,1,0:T(8,128)(2,1)} %param.13) | copy-start | bytes 196612
  239.3 1.1 copy-start.4
  240.4 74.7 %all-to-all-start.4 = ((bf16[16,8,48,256]{3,2,1,0:T(8,128)(2,1)}), bf16[16,8,48,256]{3,2,1,0:T(8,128)(2,1)S(1)}, u32[]{:S(2)}, u32[]{:S(2)}) async-start(bf16[16,8,48,256]{3,2,1,0:T(8,128)(2,1)} %bitcast.39), calls=%async_computation.4 | async-start | bytes 6291456 | tf_op jit(solution)/shard_map/all_to_all | solution.py:362
  315.1 1.7 copy-start.2
  316.7 52.6 %all-to-all-start.3 = ((bf16[16,2,8,16,256]{4,3,2,1,0:T(8,128)(2,1)}), bf16[16,2,8,16,256]{4,3,2,1,0:T(8,128)(2,1)S(1)}, u32[]{:S(2)}, u32[]{:S(2)}) async-start(bf16[16,2,8,16,256]{4,3,2,1,0:T(8,128)(2,1)} %get-tuple-element.11), calls=%async_computation.3 | async-start | bytes 4194304 | tf_op jit(solution)/shard_map/all_to_all | solution.py:362
  369.4 142.5 %copy-start.1 = (bf16[16,2,8,16,256]{4,3,2,1,0:T(8,128)(2,1)}, bf16[16,2,8,16,256]{4,3,2,1,0:T(8,128)(2,1)S(1)}, u32[]{:S(2)}) copy-start(bf16[16,2,8,16,256]{4,3,2,1,0:T(8,128)(2,1)S(1)} %all-to-all-done.3) | copy-start | bytes 6291460
  593.2 29.9 %all-to-all-start.6 = ((bf16[16,8,16,256]{3,2,1,0:T(8,128)(2,1)}), bf16[16,8,16,256]{3,2,1,0:T(8,128)(2,1)S(1)}, u32[]{:S(2)}, u32[]{:S(2)}) async-start(bf16[16,8,16,256]{3,2,1,0:T(8,128)(2,1)} %bitcast.16), calls=%async_computation.6 | async-start | bytes 2097152 | tf_op jit(solution)/shard_map/all_to_all | solution.py:362
  623.1 1.1 copy-start.3
